TPU v7x, 256 devices: a whole 4x4x8 slice. The times are simulated.
256 devices in a mesh: gz: 32 (over x, y, core), gy: 8 (over z).
Axes of the slice: x: 4, y: 4, z: 8, core: 2. Of those that a mesh axis runs over, the one named last changes fastest.
Arguments:
- volume: bfloat16 [4, 128, 128, 256], P(None, 'gz', 'gy'), may hold values from -6 to 6
- first_weight: bfloat16 [3, 3, 3, 4, 32], replicated, may hold values from -0.625 to 0.625
- first_bias: float32 [32], replicated, may hold values from -0.5 to 0.5
- second_weight: bfloat16 [3, 3, 3, 32, 64], replicated, may hold values from -0.21875 to 0.21875
- second_bias: float32 [64], replicated, may hold values from -0.5 to 0.5
- upstream: bfloat16 [64, 32, 2048], P('gz', None, 'gy'), may hold values from -0.079589844 to 0.079589844
Outputs:
- pooled: bfloat16 [64, 32, 2048], P('gz', None, 'gy')
- first_grad: float32 [3, 3, 3, 4, 32], replicated
- second_grad: float32 [3, 3, 3, 32, 64], replicated
All inputs are finite; a program needn't handle non-finite values.
Results may differ from a plain program's by a relative error of at most 0.0085.
The roundings to bfloat16 on the way count: a program that leaves them out, or rounds other values in their place, can miss the bound.
Values may be sent and summed in bfloat16 or wider, within the bound.
A program may use at most 128 MiB of HBM per device.

v0:
```python
import jax
import jax.numpy as jnp
from jax import lax
from jax.sharding import PartitionSpec as P

leak = 0.3


def extended(cells, sides, width):
    for axis, dim in sides:
        count = lax.axis_size(axis)
        ends = count - 1
        head = lax.slice_in_dim(cells, 0, width, axis=dim)
        tail = lax.slice_in_dim(cells, cells.shape[dim] - width, cells.shape[dim], axis=dim)
        cells = jnp.concatenate(
            [
                lax.ppermute(tail, axis, [(i, (i + 1) % count) for i in range(ends)]),
                cells,
                lax.ppermute(head, axis, [((i + 1) % count, i) for i in range(ends)]),
            ],
            axis=dim,
        )
    return cells


def leaky(value):
    return jnp.where(value > 0, value, leak * value)


def slope(value):
    return jnp.where(value > 0, 1.0, leak)


def pool(field):
    chans, depth, rows, width = field.shape
    return field.reshape(chans, depth // 2, 2, rows // 2, 2, width // 2, 2).mean(axis=(2, 4, 6))


def unpool(field):
    chans, depth, rows, width = field.shape
    spread = jnp.broadcast_to(
        field[:, :, None, :, None, :, None], (chans, depth, 2, rows, 2, width, 2)
    )
    return spread.reshape(chans, depth * 2, rows * 2, width * 2) * 0.125


def pad_width(field):
    return jnp.pad(field, ((0, 0), (0, 0), (0, 0), (1, 1)))


def convolve(padded, kernel):
    return lax.conv_general_dilated(
        padded[None],
        kernel,
        (1, 1, 1),
        "VALID",
        dimension_numbers=("NCDHW", "DHWIO", "NCDHW"),
        preferred_element_type=jnp.float32,
    )[0]


def kernel_term(padded, cotangent):
    outs, depth, rows, width = cotangent.shape
    chans = padded.shape[0]
    views = []
    for shift_d in range(3):
        for shift_r in range(3):
            for shift_w in range(3):
                views.append(
                    padded[
                        :,
                        shift_d : shift_d + depth,
                        shift_r : shift_r + rows,
                        shift_w : shift_w + width,
                    ]
                )
    patches = jnp.stack(views, axis=0).reshape(27 * chans, depth * rows * width)
    flat = cotangent.reshape(outs, depth * rows * width)
    result = lax.dot_general(
        patches, flat, (((1,), (1,)), ((), ())), preferred_element_type=jnp.float32
    )
    return result.reshape(3, 3, 3, chans, outs)


def on_device(volume, first_weight, first_bias, second_weight, second_bias, upstream):
    chans, depth, rows, width = volume.shape
    out_two = second_weight.shape[-1]
    vol_pad = pad_width(extended(volume, (("gz", 1), ("gy", 2)), 1))
    pre_one = convolve(vol_pad, first_weight) + first_bias[:, None, None, None]
    act_one = pool(leaky(pre_one)).astype(jnp.bfloat16)
    act_pad = pad_width(extended(act_one, (("gz", 1), ("gy", 2)), 1))
    pre_two = convolve(act_pad, second_weight) + second_bias[:, None, None, None]
    act_two = pool(leaky(pre_two)).astype(jnp.bfloat16)
    quart_d, quart_r, quart_w = (depth // 4, rows // 4, width // 4)
    pooled = lax.all_to_all(
        act_two.reshape(out_two, quart_d, quart_r * quart_w),
        "gz",
        split_axis=0,
        concat_axis=1,
        tiled=True,
    )
    back = lax.all_to_all(upstream, "gz", split_axis=1, concat_axis=0, tiled=True).reshape(
        out_two, quart_d, quart_r, quart_w
    )
    grad_two = unpool(back) * slope(pre_two)
    grad_pad = extended(grad_two, (("gz", 1), ("gy", 2)), 1)
    grad_pad = pad_width(grad_pad)
    second_term = kernel_term(act_pad, grad_two)
    turned = jnp.transpose(second_weight[::-1, ::-1, ::-1], (0, 1, 2, 4, 3))
    grad_act = convolve(grad_pad, turned)
    grad_one = (unpool(grad_act) * slope(pre_one)).astype(jnp.bfloat16)
    first_term = kernel_term(vol_pad, grad_one)
    first_total, second_total = lax.psum((first_term, second_term), ("gz", "gy"))
    return (pooled, first_total, second_total)


def solution(mesh):
    placed = (P(None, "gz", "gy", None), P(), P(), P(), P(), P("gz", None, "gy"))
    return jax.shard_map(
        on_device,
        mesh=mesh,
        in_specs=placed,
        out_specs=(P("gz", None, "gy"), P(), P()),
        check_vma=False,
    )
```

profile of v0, /device:TPU:1, one launch (start us, length us, event | category | flops | bytes accessed | tf_op | source)
XLA Modules:
  0.0 484.2 jit_solution(18221606324518688665)
XLA Ops:
  7.2 0.8 fusion.130
  8.0 4.6 collective-permute-start
  12.6 1.9 collective-permute-start.1
  14.5 1.4 copy.312
  15.9 7.6 %all-to-all-start.1 = ((bf16[2,32,256]{2,0,1:T(2,128)(2,1)}), bf16[2,32,256]{2,0,1:T(2,128)(2,1)S(1)}, u32[]{:S(2)}, u32[]{:S(2)}) async-start(bf16[2,32,256]{2,0,1:T(2,128)(2,1)} %copy.312), calls=%async_computation.1 | async-start | bytes 65536 | tf_op jit(solution)/shard_map/all_to_all | solution.py:102
  23.6 0.9 constant_dynamic-update-slice_fusion.1
  24.6 1.3 collective-permute-start.3
  25.9 4.2 collective-permute-start.2
  30.1 0.8 all-to-all-done.1
  32.0 0.8 reshape.188
  32.8 4.7 copy.299
  37.5 1.1 slice.307
  38.7 24.0 %broadcast_select_fusion = f32[4,16,8,33,32]{4,2,3,1,0:T(8,128)} fusion(pred[8,33]{0,1:T(8,128)(4,1)S(1)} %copy-done.16, bf16[3,3,3,4,32]{4,3,2,1,0:T(4,128)(2,1)S(1)} %copy-done.15, bf16[4,6,18,1,7,2]{4,0,5,2,1,3:T(4,128)(2,1)S(1)} %slice.307, bf16[4,6,18,1,8,33]{4,0,5,2,1,3:T(4,128)(2,1)} %copy.299), kind=kOutput, calls=%fused_computation.7 | convolution fusion | flops 118051584 | bytes 2410056 | tf_op jit(solution)/shard_map/conv_general_dilated | solution.py:52
  62.7 10.7 %copy.300 = f32[4,16,8,33,32]{3,2,4,1,0:T(8,128)} copy(f32[4,16,8,33,32]{4,2,3,1,0:T(8,128)} %broadcast_select_fusion) | data formatting | bytes 4325376 | tf_op jit(solution)/shard_map/conv_general_dilated | solution.py:52
  73.4 7.4 %reshape.153 = f32[4,16,1,264,32]{3,4,1,0,2:T(8,128)} reshape(f32[4,16,8,33,32]{3,2,4,1,0:T(8,128)} %copy.300) | data formatting | bytes 4325376 | tf_op jit(solution)/shard_map/conv_general_dilated | solution.py:52
  80.8 1.7 slice_bitcast_fusion
  82.6 5.0 %copy.301 = f32[1,32,4,16,256]{1,4,3,2,0:T(8,128)} copy(f32[1,32,4,16,256]{4,1,3,2,0:T(8,128)S(1)} %slice_bitcast_fusion) | data formatting | bytes 4194304 | tf_op jit(solution)/shard_map/conv_general_dilated | solution.py:52
  87.6 12.9 %fusion.2 = f32[32,2,8,128]{0,3,2,1:T(8,128)S(1)} fusion(f32[32,2,2,8,2,128,2]{0,6,5,4,3,2,1:T(2,128)} %bitcast.249, f32[32]{0:T(128)S(1)} %copy-done.12), kind=kLoop, calls=%fused_computation.4 | loop fusion | flops 2555904 | bytes 2359424 | tf_op jit(solution)/shard_map/reduce_sum | solution.py:36
  100.7 2.6 collective-permute-start.5
  103.3 14.2 %collective-permute-start.4 = (bf16[32,1,8,128]{0,3,2,1:T(8,128)(2,1)S(1)}, bf16[32,1,8,128]{0,3,2,1:T(8,128)(2,1)S(1)}, u32[]{:S(2)}, u32[]{:S(2)}) collective-permute-start(bf16[32,1,8,128]{0,3,2,1:T(8,128)(2,1)S(1)} %get-tuple-element.45), channel_id=1, source_target_pairs={{0,8},{8,16},{16,24},{24,32},{32,40},{40,48},{48,56},{56,64},{64,7... | collective-permute-start | bytes 196616 | tf_op jit(solution)/shard_map/ppermute | solution.py:17
  119.4 0.8 fusion.114
  121.5 0.8 fusion.110
  123.0 0.7 fusion.77
  123.8 0.8 fusion.108
  125.9 0.8 fusion.106
  128.0 0.8 fusion.104
  129.5 0.7 fusion.74
  130.2 0.8 fusion.102
  132.4 0.8 fusion.98
  134.5 0.8 fusion.94
  136.0 0.7 fusion.92
  137.7 1.3 collective-permute-start.7
  139.0 5.2 %collective-permute-start.6 = (bf16[32,4,1,128]{0,3,2,1:T(8,128)(2,1)}, bf16[32,4,1,128]{0,3,2,1:T(8,128)(2,1)}, u32[]{:S(2)}, u32[]{:S(2)}) collective-permute-start(bf16[32,4,1,128]{0,3,2,1:T(8,128)(2,1)} %get-tuple-element.23), channel_id=1, source_target_pairs={{0,1},{1,2},{2,3},{3,4},{4,5},{5,6},{6,7},{8,9},{9,10},{10,11},{11... | collective-permute-start | bytes 98312 | tf_op jit(solution)/shard_map/ppermute | solution.py:17
  144.2 0.8 fusion.90
  145.2 7.8 %dot_general.10 = bf16[3,3,3,4,16384]{4,3,2,1,0:T(4,128)(2,1)} reshape(bf16[27,4,4,16,256]{4,3,2,1,0:T(8,128)(2,1)} %fusion.90) | data formatting | bytes 7077888 | tf_op jit(solution)/shard_map/dot_general | solution.py:79
  153.0 0.9 copy.345
  154.3 0.8 copy.327
  155.1 0.8 copy.332
  155.8 1.0 copy.304
  156.8 1.0 copy.302
  158.5 0.9 fusion.84
  159.4 2.1 copy.369
  162.4 1.8 compare_select_fusion.2
  165.9 0.8 reduce.6
  167.4 7.8 %all-to-all-start = ((bf16[32,2,256]{2,1,0:T(2,128)(2,1)}), bf16[32,2,256]{2,1,0:T(2,128)(2,1)S(1)}, u32[]{:S(2)}, u32[]{:S(2)}) async-start(bf16[32,2,256]{2,1,0:T(2,128)(2,1)} %reshape.190), calls=%async_computation | async-start | bytes 65536 | tf_op jit(solution)/shard_map/all_to_all | solution.py:95
  175.8 0.8 fusion.127
  176.6 2.1 collective-permute-start.9
  178.8 3.6 collective-permute-start.8
  183.8 0.7 fusion.58
  187.3 0.7 copy_dynamic-update-slice_fusion.19
  195.8 0.7 copy_dynamic-update-slice_fusion.8
  198.6 0.7 copy_dynamic-update-slice_fusion.4
  202.9 6.6 %dot_general.12 = bf16[3,3,3,32,2048]{4,3,2,1,0:T(8,128)(2,1)} reshape(bf16[27,32,2,8,128]{4,3,2,1,0:T(8,128)(2,1)} %copy_dynamic-update-slice_fusion) | data formatting | bytes 7077888 | tf_op jit(solution)/shard_map/dot_general | solution.py:79
  209.5 1.3 pad_maximum_fusion.1
  211.1 1.3 collective-permute-start.11
  212.4 4.2 collective-permute-start.10
  216.6 3.9 fusion.132
  223.0 2.3 copy.370
  226.3 4.3 fusion.40
  231.2 5.6 %fusion.1 = bf16[32,2,2,8,2,128,2]{0,6,5,4,3,2,1:T(2,128)(2,1)S(1)} fusion(f32[32,2,2,8,2,128,2]{0,6,5,4,3,2,1:T(2,128)S(1)} %bitcast.252, f32[32,2,8,128]{0,3,2,1:T(8,128)S(1)} %copy.323, f32[32]{0:T(128)S(1)} %copy-done.12), kind=kLoop, calls=%fused_computation.3 | loop fusion | flops 2621440 | bytes 3408000 | tf_op jit(solution)/shard_map/convert_element_type | solution.py:111
  236.8 2.4 fusion.131
  239.2 83.6 %psum.14 = f32[3,3,3,4,32]{4,3,2,1,0:T(4,128)} all-reduce(f32[3,3,3,4,32]{4,3,2,1,0:T(4,128)S(1)} %fusion.131), channel_id=1, replica_groups=mesh['gz'=32,'gy'=8] {'gz','gy'}, use_global_device_ids=true, to_apply=%region_3.4 | all-reduce | flops 3456 | bytes 27648 | tf_op jit(solution)/shard_map/psum | solution.py:113
  322.8 152.4 %all-reduce.5.cloned.1.call-done = f32[3,3,3,32,64]{4,3,2,1,0:T(8,128)} async-done(((f32[3,3,3,32,64]{4,3,2,1,0:T(8,128)}), f32[3,3,3,32,64]{4,3,2,1,0:T(8,128)}) %all-reduce.5.cloned.1.call-update) | async-done | bytes 221200 | tf_op jit(solution)/shard_map/psum | solution.py:113
  475.1 1.8 copy.451
  (149 shorter events, 40.0 us)
Async XLA Ops:
  7.2 155.2 %copy-start = (bf16[3,3,3,32,64]{4,3,2,1,0:T(8,128)(2,1)S(1)}, bf16[3,3,3,32,64]{4,3,2,1,0:T(8,128)(2,1)}, u32[]{:S(2)}) copy-start(bf16[3,3,3,32,64]{4,3,2,1,0:T(8,128)(2,1)} %param.9) | copy-start | bytes 331780
  8.0 15.6 %collective-permute-start = (bf16[4,1,16,256]{3,2,1,0:T(8,128)(2,1)S(1)}, bf16[4,1,16,256]{3,2,1,0:T(8,128)(2,1)S(1)}, u32[]{:S(2)}, u32[]{:S(2)}) collective-permute-start(bf16[4,1,16,256]{3,2,1,0:T(8,128)(2,1)S(1)} %get-tuple-element.59), channel_id=1, source_target_pairs={{0,8},{8,16},{16,24},{24,32},{32,40},{40,48},{48,56},{56,64},{64,7... | collective-permute-start | bytes 98312 | tf_op jit(solution)/shard_map/ppermute | solution.py:17
  12.6 11.9 %collective-permute-start.1 = (bf16[4,1,16,256]{3,2,1,0:T(8,128)(2,1)S(1)}, bf16[4,1,16,256]{3,2,1,0:T(8,128)(2,1)S(1)}, u32[]{:S(2)}, u32[]{:S(2)}) collective-permute-start(bf16[4,1,16,256]{3,2,1,0:T(8,128)(2,1)S(1)} %get-tuple-element.58), channel_id=1, source_target_pairs={{8,0},{16,8},{24,16},{32,24},{40,32},{48,40},{56,48},{64,56},{72,6... | collective-permute-start | bytes 98312 | tf_op jit(solution)/shard_map/ppermute | solution.py:19
  15.9 14.9 %all-to-all-start.1 = ((bf16[2,32,256]{2,0,1:T(2,128)(2,1)}), bf16[2,32,256]{2,0,1:T(2,128)(2,1)S(1)}, u32[]{:S(2)}, u32[]{:S(2)}) async-start(bf16[2,32,256]{2,0,1:T(2,128)(2,1)} %copy.312), calls=%async_computation.1 | async-start | bytes 65536 | tf_op jit(solution)/shard_map/all_to_all | solution.py:102
  24.6 6.9 %collective-permute-start.3 = (bf16[4,6,1,256]{3,2,1,0:T(2,128)(2,1)S(1)}, bf16[4,6,1,256]{3,2,1,0:T(2,128)(2,1)S(1)}, u32[]{:S(2)}, u32[]{:S(2)}) collective-permute-start(bf16[4,6,1,256]{3,2,1,0:T(2,128)(2,1)S(1)} %get-tuple-element.57), channel_id=1, source_target_pairs={{1,0},{2,1},{3,2},{4,3},{5,4},{6,5},{7,6},{9,8},{10,9},{11,10},{12... | collective-permute-start | bytes 36872 | tf_op jit(solution)/shard_map/ppermute | solution.py:19
  25.9 5.6 %collective-permute-start.2 = (bf16[4,6,1,256]{3,2,1,0:T(2,128)(2,1)S(1)}, bf16[4,6,1,256]{3,2,1,0:T(2,128)(2,1)S(1)}, u32[]{:S(2)}, u32[]{:S(2)}) collective-permute-start(bf16[4,6,1,256]{3,2,1,0:T(2,128)(2,1)S(1)} %get-tuple-element.56), channel_id=1, source_target_pairs={{0,1},{1,2},{2,3},{3,4},{4,5},{5,6},{6,7},{8,9},{9,10},{10,11},{11... | collective-permute-start | bytes 36872 | tf_op jit(solution)/shard_map/ppermute | solution.py:17
  31.1 0.8 copy-start.3
  31.9 6.7 %copy-start.15 = (bf16[3,3,3,4,32]{4,3,2,1,0:T(4,128)(2,1)S(1)}, bf16[3,3,3,4,32]{4,3,2,1,0:T(4,128)(2,1)}, u32[]{:S(2)}) copy-start(bf16[3,3,3,4,32]{4,3,2,1,0:T(4,128)(2,1)} %param.7) | copy-start | bytes 20740
  32.0 6.7 %copy-start.16 = (pred[8,33]{0,1:T(8,128)(4,1)S(1)}, pred[8,33]{0,1:T(8,128)(4,1)}, u32[]{:S(2)}) copy-start(pred[8,33]{0,1:T(8,128)(4,1)} %constant.42) | copy-start | bytes 796
  82.6 5.0 %copy-start.12 = (f32[32]{0:T(128)S(1)}, f32[32]{0:T(128)}, u32[]{:S(2)}) copy-start(f32[32]{0:T(128)} %param.8) | copy-start | bytes 388
  100.4 20.4 %copy-start.2 = (bf16[4,4,16,256]{3,2,1,0:T(8,128)(2,1)S(1)}, bf16[4,4,16,256]{3,2,1,0:T(8,128)(2,1)}, u32[]{:S(2)}) copy-start(bf16[4,4,16,256]{3,2,1,0:T(8,128)(2,1)} %param.6) | copy-start | bytes 393220
  100.7 36.0 %collective-permute-start.5 = (bf16[32,1,8,128]{0,3,2,1:T(8,128)(2,1)S(1)}, bf16[32,1,8,128]{0,3,2,1:T(8,128)(2,1)S(1)}, u32[]{:S(2)}, u32[]{:S(2)}) collective-permute-start(bf16[32,1,8,128]{0,3,2,1:T(8,128)(2,1)S(1)} %get-tuple-element.46), channel_id=1, source_target_pairs={{8,0},{16,8},{24,16},{32,24},{40,32},{48,40},{56,48},{64,56},{72,6... | collective-permute-start | bytes 196616 | tf_op jit(solution)/shard_map/ppermute | solution.py:19
  103.3 33.4 %collective-permute-start.4 = (bf16[32,1,8,128]{0,3,2,1:T(8,128)(2,1)S(1)}, bf16[32,1,8,128]{0,3,2,1:T(8,128)(2,1)S(1)}, u32[]{:S(2)}, u32[]{:S(2)}) collective-permute-start(bf16[32,1,8,128]{0,3,2,1:T(8,128)(2,1)S(1)} %get-tuple-element.45), channel_id=1, source_target_pairs={{0,8},{8,16},{16,24},{24,32},{32,40},{40,48},{48,56},{56,64},{64,7... | collective-permute-start | bytes 196616 | tf_op jit(solution)/shard_map/ppermute | solution.py:17
  137.7 18.1 %collective-permute-start.7 = (bf16[32,4,1,128]{0,3,2,1:T(8,128)(2,1)}, bf16[32,4,1,128]{0,3,2,1:T(8,128)(2,1)}, u32[]{:S(2)}, u32[]{:S(2)}) collective-permute-start(bf16[32,4,1,128]{0,3,2,1:T(8,128)(2,1)} %get-tuple-element.24), channel_id=1, source_target_pairs={{1,0},{2,1},{3,2},{4,3},{5,4},{6,5},{7,6},{9,8},{10,9},{11,10},{12... | collective-permute-start | bytes 98312 | tf_op jit(solution)/shard_map/ppermute | solution.py:19
  139.0 17.8 %collective-permute-start.6 = (bf16[32,4,1,128]{0,3,2,1:T(8,128)(2,1)}, bf16[32,4,1,128]{0,3,2,1:T(8,128)(2,1)}, u32[]{:S(2)}, u32[]{:S(2)}) collective-permute-start(bf16[32,4,1,128]{0,3,2,1:T(8,128)(2,1)} %get-tuple-element.23), channel_id=1, source_target_pairs={{0,1},{1,2},{2,3},{3,4},{4,5},{5,6},{6,7},{8,9},{9,10},{10,11},{11... | collective-permute-start | bytes 98312 | tf_op jit(solution)/shard_map/ppermute | solution.py:17
  159.4 3.0 copy-start.13
  159.4 3.1 copy-start.17
  164.5 11.1 %copy-start.14 = (f32[64]{0:T(128)S(1)}, f32[64]{0:T(128)}, u32[]{:S(2)}) copy-start(f32[64]{0:T(128)} %param.10) | copy-start | bytes 772
  167.4 53.1 %all-to-all-start = ((bf16[32,2,256]{2,1,0:T(2,128)(2,1)}), bf16[32,2,256]{2,1,0:T(2,128)(2,1)S(1)}, u32[]{:S(2)}, u32[]{:S(2)}) async-start(bf16[32,2,256]{2,1,0:T(2,128)(2,1)} %reshape.190), calls=%async_computation | async-start | bytes 65536 | tf_op jit(solution)/shard_map/all_to_all | solution.py:95
  175.2 299.9 %all-reduce.5.cloned.1.call-start = ((), (), s32[]{:S(2)}) async-start(), calls=%async_computation.2 | async-start | bytes 884736 | tf_op jit(solution)/shard_map/psum | solution.py:113
  176.6 32.9 %collective-permute-start.9 = (bf16[64,1,8,128]{0,2,3,1:T(8,128)(2,1)}, bf16[64,1,8,128]{0,2,3,1:T(8,128)(2,1)}, u32[]{:S(2)}, u32[]{:S(2)}) collective-permute-start(bf16[64,1,8,128]{0,2,3,1:T(8,128)(2,1)} %get-tuple-element.44), channel_id=1, source_target_pairs={{8,0},{16,8},{24,16},{32,24},{40,32},{48,40},{56,48},{64,56},{72,6... | collective-permute-start | bytes 393224 | tf_op jit(solution)/shard_map/ppermute | solution.py:19
  178.7 5.1 %copy-start.4 = (bf16[64,4,64]{0,2,1:T(8,128)(2,1)S(1)}, bf16[64,4,64]{0,2,1:T(8,128)(2,1)}, u32[]{:S(2)}) copy-start(bf16[64,4,64]{0,2,1:T(8,128)(2,1)} %copy-done.3) | copy-start | bytes 98308
  178.8 5.8 %copy-start.9 = (bf16[1,32,2,8,128]{4,1,3,2,0:T(8,128)(2,1)S(1)}, bf16[1,32,2,8,128]{4,1,3,2,0:T(8,128)(2,1)}, u32[]{:S(2)}) copy-start(bf16[1,32,2,8,128]{4,1,3,2,0:T(8,128)(2,1)} %get-tuple-element.54) | copy-start | bytes 393220
  178.8 30.7 %collective-permute-start.8 = (bf16[64,1,8,128]{0,2,3,1:T(8,128)(2,1)}, bf16[64,1,8,128]{0,2,3,1:T(8,128)(2,1)}, u32[]{:S(2)}, u32[]{:S(2)}) collective-permute-start(bf16[64,1,8,128]{0,2,3,1:T(8,128)(2,1)} %get-tuple-element.43), channel_id=1, source_target_pairs={{0,8},{8,16},{16,24},{24,32},{32,40},{40,48},{48,56},{56,64},{64,7... | collective-permute-start | bytes 393224 | tf_op jit(solution)/shard_map/ppermute | solution.py:17
  182.8 3.8 copy-start.11
  182.9 5.9 %copy-start.8 = (bf16[1,32,2,8,128]{4,1,3,2,0:T(8,128)(2,1)S(1)}, bf16[1,32,2,8,128]{4,1,3,2,0:T(8,128)(2,1)}, u32[]{:S(2)}) copy-start(bf16[1,32,2,8,128]{4,1,3,2,0:T(8,128)(2,1)} %get-tuple-element.48) | copy-start | bytes 393220
  182.9 8.0 %copy-start.7 = (bf16[1,32,2,8,128]{4,1,3,2,0:T(8,128)(2,1)S(1)}, bf16[1,32,2,8,128]{4,1,3,2,0:T(8,128)(2,1)}, u32[]{:S(2)}) copy-start(bf16[1,32,2,8,128]{4,1,3,2,0:T(8,128)(2,1)} %get-tuple-element.53) | copy-start | bytes 393220
  183.6 9.4 %copy-start.5 = (bf16[1,32,2,8,128]{4,3,2,1,0:T(8,128)(2,1)S(1)}, bf16[1,32,2,8,128]{4,3,2,1,0:T(8,128)(2,1)}, u32[]{:S(2)}) copy-start(bf16[1,32,2,8,128]{4,3,2,1,0:T(8,128)(2,1)} %copy.345) | copy-start | bytes 393220
  183.6 11.5 %copy-start.6 = (bf16[1,32,2,8,128]{4,1,3,2,0:T(8,128)(2,1)S(1)}, bf16[1,32,2,8,128]{4,1,3,2,0:T(8,128)(2,1)}, u32[]{:S(2)}) copy-start(bf16[1,32,2,8,128]{4,1,3,2,0:T(8,128)(2,1)} %get-tuple-element.49) | copy-start | bytes 393220
  183.8 15.6 %copy-start.10 = (bf16[32,1,8,128]{3,2,1,0:T(8,128)(2,1)S(1)}, bf16[32,1,8,128]{3,2,1,0:T(8,128)(2,1)}, u32[]{:S(2)}) copy-start(bf16[32,1,8,128]{3,2,1,0:T(8,128)(2,1)} %copy.332) | copy-start | bytes 196612
  211.1 10.9 %collective-permute-start.11 = (bf16[64,4,1,128]{0,2,3,1:T(2,128)(2,1)S(1)}, bf16[64,4,1,128]{0,2,3,1:T(2,128)(2,1)S(1)}, u32[]{:S(2)}, u32[]{:S(2)}) collective-permute-start(bf16[64,4,1,128]{0,2,3,1:T(2,128)(2,1)S(1)} %get-tuple-element.22), channel_id=1, source_target_pairs={{1,0},{2,1},{3,2},{4,3},{5,4},{6,5},{7,6},{9,8},{10,9},{11,10},{12... | collective-permute-start | bytes 196616 | tf_op jit(solution)/shard_map/ppermute | solution.py:19
  212.4 9.8 %collective-permute-start.10 = (bf16[64,4,1,128]{0,2,3,1:T(2,128)(2,1)S(1)}, bf16[64,4,1,128]{0,2,3,1:T(2,128)(2,1)S(1)}, u32[]{:S(2)}, u32[]{:S(2)}) collective-permute-start(bf16[64,4,1,128]{0,2,3,1:T(2,128)(2,1)S(1)} %get-tuple-element.21), channel_id=1, source_target_pairs={{0,1},{1,2},{2,3},{3,4},{4,5},{5,6},{6,7},{8,9},{9,10},{10,11},{11... | collective-permute-start | bytes 196616 | tf_op jit(solution)/shard_map/ppermute | solution.py:17
  225.3 1.0 copy-start.18
  226.2 4.9 %slice-start = ((s8[8388608]{0:T(1024)(128)(4,1)}), s8[4194304]{0:T(1024)(128)(4,1)S(1)}, s32[]{:S(2)}) async-start(s8[8388608]{0:T(1024)(128)(4,1)} %bitcast.250), calls=%async_computation.3 | async-start | bytes 8388608
  226.3 4.9 %slice-start.1 = ((s8[8388608]{0:T(1024)(128)(4,1)}), s8[4194304]{0:T(1024)(128)(4,1)S(1)}, s32[]{:S(2)}) async-start(s8[8388608]{0:T(1024)(128)(4,1)} %bitcast.250), calls=%async_computation.4 | async-start | bytes 8388608
  231.2 5.6 %copy-start.1 = (bf16[3,3,3,4,16384]{4,3,2,1,0:T(4,128)(2,1)S(1)}, bf16[3,3,3,4,16384]{4,3,2,1,0:T(4,128)(2,1)}, u32[]{:S(2)}) copy-start(bf16[3,3,3,4,16384]{4,3,2,1,0:T(4,128)(2,1)} %dot_general.10) | copy-start | bytes 10616836
Sparse Core Ops, SparseCore 0:
  220.6 254.4 all-reduce.4
where the time goes:
time: 494 us; the launch traced here: 484 us
  waiting for transfers between devices  153 us (31%)
  local copies, waits for them, and re-layouts  101 us (20%)
  blocking collectives  83.6 us (17%)
  starting transfers between devices  62 us (13%)
  matrix products  36.4 us (7%)
  other arithmetic  32.8 us (7%)
  between operations  15.3 us (3%)
    psum x1, waiting for transfers between devices, on_device(): lax.psum((first_term, second_term), ('gz', 'gy'))  152 us
    psum x1, blocking collectives, on_device(): lax.psum((first_term, second_term), ('gz', 'gy'))  83.6 us
    unnamed x93, local copies, waits for them, and re-layouts  39.9 us
    ppermute x6, starting transfers between devices, extended(): lax.ppermute(tail, axis, [(i, (i + 1) % count) for i in range(ends)])  36 us
    conv_general_dilated x14, local copies, waits for them, and re-layouts, convolve(): lax.conv_general_dilated(padded[None], kernel, (1, 1, 1), 'VALID', dimens...  32.4 us
    conv_general_dilated x3, matrix products, convolve(): lax.conv_general_dilated(padded[None], kernel, (1, 1, 1), 'VALID', dimens...  30.1 us
    dot_general x2, local copies, waits for them, and re-layouts, kernel_term(): lax.dot_general(patches, flat, (((1,), (1,)), ((), ())), preferred_elemen...  14.4 us
    reduce_sum x3, other arithmetic, pool(): field.reshape(chans, depth // 2, 2, rows // 2, 2, width // 2, 2)  13.5 us
  transfers between devices with their start and end apart: 15, of which 2 were waited for; matrix products, arithmetic and copies ran while one was open for 18% of the time, Pallas kernels for 0%

commit v1 on v0

v1 whole, which is shorter than its diff:
```python
import functools

import jax
import jax.numpy as jnp
import numpy as np
from jax import lax
from jax.experimental import pallas as pl
from jax.experimental.pallas import tpu as pltpu
from jax.sharding import PartitionSpec as P

LEAK = 0.3
F32 = jnp.float32
BF16 = jnp.bfloat16
MESH = pl.DeviceIdType.MESH
VMEM = pl.BlockSpec(memory_space=pltpu.VMEM)
GZ, GY = 32, 8
LIMIT = 56 * 2**20


def lanes_of(shape):
    return lax.broadcasted_iota(jnp.int32, shape, len(shape) - 1)


def before(x):
    lane = lanes_of(x.shape)
    return jnp.where(lane >= 64, pltpu.roll(x, 64, 1), jnp.where(lane == 0, 0.0, pltpu.roll(x, 65, 1)))


def after(x):
    lane = lanes_of(x.shape)
    return jnp.where(lane < 64, pltpu.roll(x, 64, 1), jnp.where(lane == 127, 0.0, pltpu.roll(x, 63, 1)))


def mm(a, b):
    return jnp.dot(a, b, preferred_element_type=F32)


def mm_nt(a, b):
    return lax.dot_general(a, b, (((1,), (1,)), ((), ())), preferred_element_type=F32)


def place():
    return lax.axis_index("gz"), lax.axis_index("gy")


def spread_matrix():
    out = np.zeros((256, 4, 128), np.float32)
    for lane in range(128):
        cell = 2 * (lane % 64) + lane // 64
        for dw in range(4):
            w = 2 * cell + dw - 1
            if 0 <= w < 256:
                out[w, dw, lane] = 1
    return out.reshape(256, 512).astype(jnp.bfloat16)


def channel_matrix():
    out = np.zeros((64, 64), np.float32)
    for q in range(64):
        out[q, (q % 2) * 32 + q // 2] = 1
    return out.astype(jnp.bfloat16)


def gather_matrix():
    out = np.zeros((2, 2, 2, 4, 4, 4, 4, 128), np.float32)
    for pd in range(2):
        for pr in range(2):
            for pw in range(2):
                for r in range(3):
                    for s in range(3):
                        for t in range(3):
                            for c in range(4):
                                out[pd, pr, pw, pd + r, pw + t, pr + s, c, ((r * 3 + s) * 3 + t) * 4 + c] = 1
    return out.reshape(2048, 128).astype(jnp.bfloat16)


def partners(gz, gy, dz, dy):
    return lax.rem(gz + dz + GZ, GZ), lax.rem(gy + dy + GY, GY)


def exchange_in(vol_ref, up_ref, ext_ref, back_ref, land, stage, got, send, recv, a_send, a_recv):
    gz, gy = place()
    for half in range(2):
        for chan in range(2):
            stage[pl.ds(chan * 2 + half, GZ, stride=8), :] = up_ref[chan, :, half * 128 : half * 128 + 128].astype(F32)
    copies = []
    number = 0
    for dz in (-1, 0, 1):
        src_d, dst_d = {-1: (slice(0, 3), slice(7, 10)), 0: (slice(0, 4), slice(3, 7)), 1: (slice(1, 4), slice(0, 3))}[dz]
        for dy in (-1, 0, 1):
            if dz == 0 and dy == 0:
                continue
            src_r, dst_r = {
                -1: (slice(0, 16), slice(80, 96)),
                0: (slice(0, 64), slice(16, 80)),
                1: (slice(48, 64), slice(0, 16)),
            }[dy]
            copy = pltpu.make_async_remote_copy(
                src_ref=vol_ref.at[src_d, src_r],
                dst_ref=land.at[dst_d, dst_r],
                send_sem=send.at[number],
                recv_sem=recv.at[number],
                device_id=partners(gz, gy, dz, dy),
                device_id_type=MESH,
            )
            copy.start()
            copies.append(copy)
            number += 1

    def scatter(k, _):
        to = lax.rem(gz + k, GZ)
        pltpu.make_async_remote_copy(
            src_ref=stage.at[pl.ds(pl.multiple_of(to * 8, 8), 8)],
            dst_ref=got.at[pl.ds(pl.multiple_of(gz * 8, 8), 8)],
            send_sem=a_send,
            recv_sem=a_recv,
            device_id=(to, gy),
            device_id_type=MESH,
        ).start()
        return 0

    lax.fori_loop(1, GZ, scatter, 0)
    land[3:7, 16:80] = vol_ref[...]
    mine = pl.ds(pl.multiple_of(gz * 8, 8), 8)
    for copy in copies:
        copy.wait()
    whole = pltpu.make_async_remote_copy(
        src_ref=stage.at[pl.ds(0, 8 * GZ - 8)],
        dst_ref=got.at[pl.ds(0, 8 * GZ - 8)],
        send_sem=a_send,
        recv_sem=a_recv,
        device_id=(lax.rem(gz + 1, GZ), gy),
        device_id_type=MESH,
    )
    whole.wait()
    got[mine, :] = stage[mine, :]
    row = lax.broadcasted_iota(jnp.int32, (10, 96, 256), 1)
    dep = lax.broadcasted_iota(jnp.int32, (10, 96, 256), 0)
    low_d = jnp.where(gz == 0, 3, 0)
    high_d = jnp.where(gz == GZ - 1, 7, 10)
    low_r = jnp.where(gy == 0, 16, 0)
    high_r = jnp.where(gy == GY - 1, 80, 96)
    inside = (dep >= low_d) & (dep < high_d) & (row >= low_r) & (row < high_r)
    ext_ref[...] = jnp.where(inside, land[...].astype(F32), 0.0).astype(BF16)
    for half in range(2):
        for chan in range(2):
            back_ref[chan * 32 : chan * 32 + 32, half * 128 : half * 128 + 128] = got[
                pl.ds(chan * 2 + half, GZ, stride=8), :
            ].astype(BF16)


def forward(
    ext_ref, back_ref, w1_ref, b1_ref, w2_ref, b2_ref, spread_ref, chan_ref,
    patch_ref, pre_ref, grad_ref, pool_ref, sg_ref, rows, act, full,
):
    gz, gy = place()
    for d in range(10):
        wide = mm(ext_ref[d], spread_ref[...])
        for dw in range(4):
            rows[d, dw] = wide[:, dw * 128 : dw * 128 + 128]

    def window(d, _):
        for dd in range(4):
            for dw in range(4):
                for r in range(10):
                    patch_ref[d, dd * 64 + dw * 16 : dd * 64 + dw * 16 + 16, r * 128 : r * 128 + 128] = rows[
                        2 * d + dd, dw, 8 * r + 4 : 8 * r + 20, :
                    ].astype(BF16)
        return 0

    lax.fori_loop(0, 4, window, 0)

    def layer_one(d, _):
        d_in = jnp.where(d == 0, gz > 0, jnp.where(d == 3, gz < GZ - 1, True))
        for j in range(5):
            pre = mm(w1_ref[...], patch_ref[d, :, j * 256 : j * 256 + 256]) + b1_ref[...]
            pre_ref[d, :, j * 256 : j * 256 + 256] = pre.astype(BF16)
            out = jnp.maximum(pre, LEAK * pre)
            cell = out[0:32]
            for g in range(1, 8):
                cell = cell + out[g * 32 : g * 32 + 32]
            cell = (cell * 0.125).astype(BF16).astype(F32)
            for k in range(2):
                r = 2 * j + k
                ok = d_in
                if r == 0:
                    ok = ok & (gy > 0)
                if r == 9:
                    ok = ok & (gy < GY - 1)
                one = jnp.where(ok, cell[:, k * 128 : k * 128 + 128], 0.0)
                act[d, 0, r * 32 : r * 32 + 32, :] = before(one).astype(BF16)
                act[d, 1, r * 32 : r * 32 + 32, :] = one.astype(BF16)
                act[d, 2, r * 32 : r * 32 + 32, :] = after(one).astype(BF16)
        return 0

    lax.fori_loop(0, 4, layer_one, 0)
    back = mm(chan_ref[...], back_ref[...])
    lane = lanes_of((64, 128))
    for h in range(2):
        sides = []
        for k in range(2):
            r = 4 * h + 2 * k
            sides.append(
                jnp.concatenate([act[dd, dw, r * 32 : r * 32 + 128, :] for dd in range(4) for dw in range(3)], axis=0)
            )
        patches = jnp.concatenate(sides, axis=1)
        pre = mm(w2_ref[...], patches) + b2_ref[...]
        out = jnp.maximum(pre, LEAK * pre)
        cell = out[0:64] + out[64:128] + out[128:192] + out[192:256]
        left, right = cell[:, :128], cell[:, 128:]
        left = left + pltpu.roll(left, 64, 1)
        right = right + pltpu.roll(right, 64, 1)
        pooled = (jnp.where(lane < 64, left, right) * 0.125).astype(BF16)
        pool_ref[:, h * 128 : h * 128 + 128] = pooled
        up = back[:, h * 128 : h * 128 + 128] * 0.125
        other = pltpu.roll(up, 64, 1)
        both = jnp.concatenate([jnp.where(lane < 64, up, other), jnp.where(lane < 64, other, up)], axis=1)
        weak = both * LEAK
        parts = []
        for g in range(4):
            part = jnp.where(pre[g * 64 : g * 64 + 64] > 0, both, weak).astype(BF16)
            parts.append(part)
            for k in range(2):
                grad_ref[g // 2, 4 * h + 2 * k + g % 2] = part[:, k * 128 : k * 128 + 128]
        term = mm_nt(patches, jnp.concatenate(parts, axis=0))
        if h == 0:
            full[...] = term
        else:
            full[...] += term
    lane = lanes_of((16, 128))
    for r in range(3):
        for t in range(3):
            near = []
            for dr in range(4):
                a = ((r * 3 + t) * 4 + dr) * 32
                b = (((r + 1) * 3 + t) * 4 + dr) * 32
                near.append(full[a : a + 32, 0:128] + full[b : b + 32, 128:256])
            for s in range(3):
                low = near[s][:16] + pltpu.roll(near[s + 1][:16], 64, 1)
                high = pltpu.roll(near[s][16:], 64, 1) + near[s + 1][16:]
                at = ((r * 3 + s) * 3 + t) * 16
                sg_ref[at : at + 16, :] = jnp.where(lane < 64, low, high)
    sg_ref[432:512, :] = jnp.zeros((80, 128), F32)


def spread16(kind, gz, gy, k):
    if kind == 0:
        return lax.rem(gz + 2 * k, GZ), gy
    own = gy * 2 + lax.rem(gz, 2)
    other = lax.rem(own + k, 16)
    return gz - lax.rem(gz, 2) + lax.rem(other, 2), other // 2


def rank16(kind, gz, gy):
    return gz // 2 if kind == 0 else gy * 2 + lax.rem(gz, 2)


def share(kind, src_of, landing, own_slot, send, recv, one):
    gz, gy = place()

    def go(k, _):
        to = spread16(kind, gz, gy, k)
        pltpu.make_async_remote_copy(
            src_ref=src_of(rank16(kind, *to)),
            dst_ref=landing.at[own_slot],
            send_sem=send,
            recv_sem=recv,
            device_id=to,
            device_id_type=MESH,
        ).start()
        return 0

    lax.fori_loop(1, 16, go, 0)

    def wait():
        pltpu.make_async_remote_copy(
            src_ref=landing.at[pl.ds(0, 15)],
            dst_ref=landing.at[pl.ds(0, 15)],
            send_sem=send,
            recv_sem=recv,
            device_id=spread16(kind, gz, gy, 1),
            device_id_type=MESH,
        ).wait()

    return wait


def total16(landing):
    value = landing[0]
    for k in range(1, 16):
        value = value + landing[k]
    return value


def exchange_out(
    grad_ref, pool_ref, chan_ref, sg_ref, ext_ref, out_ref, total_ref,
    land, stage, got, one, two, part, done, send, recv, a_send, a_recv, s_send, s_recv,
):
    gz, gy = place()
    copies = []
    number = 0
    for dz in (-1, 0, 1):
        src_d, dst_d = {-1: (slice(0, 1), slice(3, 4)), 0: (slice(0, 2), slice(1, 3)), 1: (slice(1, 2), slice(0, 1))}[dz]
        for dy in (-1, 0, 1):
            if dz == 0 and dy == 0:
                continue
            src_r, dst_r = {-1: (slice(0, 1), slice(9, 10)), 0: (slice(0, 8), slice(1, 9)), 1: (slice(7, 8), slice(0, 1))}[dy]
            copy = pltpu.make_async_remote_copy(
                src_ref=grad_ref.at[src_d, src_r],
                dst_ref=land.at[dst_d, dst_r],
                send_sem=send.at[number],
                recv_sem=recv.at[number],
                device_id=partners(gz, gy, dz, dy),
                device_id_type=MESH,
            )
            copy.start()
            copies.append(copy)
            number += 1
    chip = rank16(0, gz, gy)
    line = rank16(1, gz, gy)
    wait_one = share(0, lambda j: sg_ref.at[pl.ds(pl.multiple_of(j * 32, 32), 32)], one, chip, s_send.at[0], s_recv.at[0], None)
    one_own = sg_ref[pl.ds(pl.multiple_of(chip * 32, 32), 32), :]
    pooled = lax.dot_general(chan_ref[...], pool_ref[...], (((0,), (0,)), ((), ())), preferred_element_type=F32)
    for half in range(2):
        for chan in range(2):
            stage[pl.ds(chan * 2 + half, GZ, stride=8), :] = pooled[chan * 32 : chan * 32 + 32, half * 128 : half * 128 + 128]

    def scatter(k, _):
        to = lax.rem(gz + k, GZ)
        pltpu.make_async_remote_copy(
            src_ref=stage.at[pl.ds(pl.multiple_of(to * 8, 8), 8)],
            dst_ref=got.at[pl.ds(pl.multiple_of(gz * 8, 8), 8)],
            send_sem=a_send,
            recv_sem=a_recv,
            device_id=(to, gy),
            device_id_type=MESH,
        ).start()
        return 0

    lax.fori_loop(1, GZ, scatter, 0)
    wait_one()
    one[chip] = one_own
    part[...] = total16(one)
    wait_two = share(1, lambda j: part, two, line, s_send.at[1], s_recv.at[1], None)
    for copy in copies:
        copy.wait()
    land[1:3, 1:9] = grad_ref[...]

    @pl.when(gz == 0)
    def _():
        land[0] = jnp.zeros((10, 64, 128), BF16)

    @pl.when(gz == GZ - 1)
    def _():
        land[3] = jnp.zeros((10, 64, 128), BF16)

    @pl.when(gy == 0)
    def _():
        land[:, 0] = jnp.zeros((4, 64, 128), BF16)

    @pl.when(gy == GY - 1)
    def _():
        land[:, 9] = jnp.zeros((4, 64, 128), BF16)

    ext_ref[...] = land[...]
    wait_two()
    two[line] = part[...]
    done[chip] = total16(two)
    wait_three = share(0, lambda j: done.at[chip], done, chip, s_send.at[2], s_recv.at[2], None)
    mine = pl.ds(pl.multiple_of(gz * 8, 8), 8)
    whole = pltpu.make_async_remote_copy(
        src_ref=stage.at[pl.ds(0, 8 * GZ - 8)],
        dst_ref=got.at[pl.ds(0, 8 * GZ - 8)],
        send_sem=a_send,
        recv_sem=a_recv,
        device_id=(lax.rem(gz + 1, GZ), gy),
        device_id_type=MESH,
    )
    whole.wait()
    got[mine, :] = stage[mine, :]
    for half in range(2):
        for chan in range(2):
            out_ref[chan, :, half * 128 : half * 128 + 128] = got[pl.ds(chan * 2 + half, GZ, stride=8), :].astype(BF16)
    wait_three()
    for j in range(27):
        block = done[j // 2, (j % 2) * 16 : (j % 2) * 16 + 16, :]
        total_ref[j * 32 : j * 32 + 16, :] = block[:, :64]
        total_ref[j * 32 + 16 : j * 32 + 32, :] = block[:, 64:]


def backward(ext_ref, patch_ref, pre_ref, w3_ref, gather_ref, out_ref, first):
    for h in range(2):
        sides = []
        for k in range(2):
            r = 4 * h + 2 * k
            sides.append(
                jnp.concatenate([ext_ref[dd, r : r + 4].reshape(256, 128) for dd in range(4)], axis=0)
            )
        spread = mm(w3_ref[...], jnp.concatenate(sides, axis=1))
        for k in range(2):
            lanes = slice(k * 128, k * 128 + 128)
            grad = after(spread[0:128, lanes]) + spread[128:256, lanes] + before(spread[256:384, lanes])
            grad = grad * 0.125
            for g in range(4):
                pd, r = g // 2, 4 * h + 2 * k + g % 2
                strong = grad[g * 32 : g * 32 + 32]
                weak = strong * LEAK
                for m in range(8):
                    pre = pre_ref[1 + pd, m * 32 : m * 32 + 32, (1 + r) * 128 : (2 + r) * 128].astype(F32)
                    first[m * 32 : m * 32 + 32, (pd * 8 + r) * 128 : (pd * 8 + r + 1) * 128] = jnp.where(
                        pre > 0, strong, weak
                    ).astype(BF16)
    full = mm_nt(first[:, :1024], patch_ref[1, :, 128:1152]) + mm_nt(first[:, 1024:], patch_ref[2, :, 128:1152])
    flat = jnp.concatenate([full[g * 32 : g * 32 + 32] for g in range(8)], axis=1)
    total = jnp.zeros((32, 128), F32)
    for _ in range(3):
        piece = flat.astype(BF16)
        total = total + mm(piece, gather_ref[...])
        flat = flat - piece.astype(F32)
    out_ref[...] = total


def sum_first(term_ref, out_ref, one, two, part, send, recv):
    gz, gy = place()
    chip, line = rank16(0, gz, gy), rank16(1, gz, gy)
    wait_one = share(0, lambda j: term_ref, one, chip, send.at[0], recv.at[0], None)
    wait_one()
    one[chip] = term_ref[...]
    part[...] = total16(one)
    wait_two = share(1, lambda j: part, two, line, send.at[1], recv.at[1], None)
    wait_two()
    two[line] = part[...]
    out_ref[...] = total16(two)


def kernel_call(body, outs, scratch, remote, *operands):
    return pl.pallas_call(
        body,
        out_shape=[jax.ShapeDtypeStruct(shape, dtype) for shape, dtype in outs],
        in_specs=[VMEM] * len(operands),
        out_specs=[VMEM] * len(outs),
        scratch_shapes=scratch,
        compiler_params=pltpu.CompilerParams(vmem_limit_bytes=LIMIT, has_side_effects=remote),
    )(*operands)


def prepare(first_weight, second_weight):
    turned = jnp.transpose(first_weight, (4, 0, 2, 1, 3))
    first = [
        jnp.pad(turned, ((0, 0), (pd, 1 - pd), (pw, 1 - pw), (pr, 1 - pr), (0, 0)))
        for pd in range(2)
        for pr in range(2)
        for pw in range(2)
    ]
    first = jnp.stack(first).reshape(256, 256)
    turned = jnp.transpose(second_weight, (4, 0, 2, 1, 3))
    second = [
        jnp.pad(turned, ((0, 0), (pd, 1 - pd), (0, 0), (pr, 1 - pr), (0, 0))) for pd in range(2) for pr in range(2)
    ]
    second = jnp.stack(second).reshape(256, 1536)
    turned = jnp.transpose(second_weight[::-1, ::-1], (2, 3, 0, 1, 4))
    third = [
        jnp.pad(turned, ((0, 0), (0, 0), (pd, 1 - pd), (pr, 1 - pr), (0, 0))) for pd in range(2) for pr in range(2)
    ]
    third = jnp.stack(third, axis=1).reshape(384, 1024)
    return first, second, third


def on_device(volume, first_weight, first_bias, second_weight, second_bias, upstream):
    dma, sem = pltpu.SemaphoreType.DMA, pltpu.VMEM
    w1, w2, w3 = prepare(first_weight, second_weight)
    b1 = jnp.tile(first_bias, 8)[:, None]
    b2 = jnp.tile(second_bias, 4)[:, None]
    spread = jnp.asarray(spread_matrix())
    chan = jnp.asarray(channel_matrix())
    gather = jnp.asarray(gather_matrix())
    own = jnp.transpose(volume, (1, 2, 0, 3)).reshape(4, 64, 256)
    ext, back = kernel_call(
        exchange_in,
        [((10, 96, 256), BF16), ((64, 256), BF16)],
        [sem((10, 96, 256), BF16), sem((256, 128), F32), sem((256, 128), F32), dma((8,)), dma((8,)), dma, dma],
        True, own, upstream,
    )
    patch, pre, grad, pool, sg = kernel_call(
        forward,
        [((4, 256, 1280), BF16), ((4, 256, 1280), BF16), ((2, 8, 64, 128), BF16), ((64, 256), BF16), ((512, 128), F32)],
        [sem((10, 4, 96, 128), F32), sem((4, 3, 320, 128), BF16), sem((1536, 256), F32)],
        False, ext, back, w1, b1, w2, b2, spread, chan,
    )
    grads, pooled, second = kernel_call(
        exchange_out,
        [((4, 10, 64, 128), BF16), ((2, 32, 256), BF16), ((864, 64), F32)],
        [
            sem((4, 10, 64, 128), BF16), sem((256, 128), F32), sem((256, 128), F32), sem((16, 32, 128), F32),
            sem((16, 32, 128), F32), sem((32, 128), F32), sem((16, 32, 128), F32),
            dma((8,)), dma((8,)), dma, dma, dma((3,)), dma((3,)),
        ],
        True, grad, pool, chan, sg,
    )
    (term,) = kernel_call(backward, [((32, 128), F32)], [sem((256, 2048), BF16)], False, grads, patch, pre, w3, gather)
    (first,) = kernel_call(
        sum_first,
        [((32, 128), F32)],
        [sem((16, 32, 128), F32), sem((16, 32, 128), F32), sem((32, 128), F32), dma((2,)), dma((2,))],
        True, term,
    )
    first = jnp.transpose(first[:, :108]).reshape(3, 3, 3, 4, 32)
    return pooled, first, second.reshape(3, 3, 3, 32, 64)


def solution(mesh):
    placed = (P(None, "gz", "gy", None), P(), P(), P(), P(), P("gz", None, "gy"))
    return jax.shard_map(
        on_device,
        mesh=mesh,
        in_specs=placed,
        out_specs=(P("gz", None, "gy"), P(), P()),
        check_vma=False,
    )
```

time: 494 us -> 125 us (0.25); the launches traced: 484 us -> 124 us
  waiting for transfers between devices: 153 us -> 0 us
  Pallas kernels: 0 us -> 104 us
  blocking collectives: 83.6 us -> 0 us
  local copies, waits for them, and re-layouts: 101 us -> 18.5 us
  starting transfers between devices: 62 us -> 0 us
  matrix products: 36.4 us -> 0 us
  other arithmetic: 32.8 us -> 0.82 us
  between operations: 15.3 us -> 0.8 us
    psum x1 -> x0, waiting for transfers between devices: 152 us -> none  [on_device(): lax.psum((first_term, second_term), ('gz', 'gy'))]
    pallas_call x0 -> x5, Pallas kernels: none -> 104 us  [kernel_call(): pl.pallas_call(body, out_shape=[jax.ShapeDtypeStruct(shape, dtype) for sh...]
    psum x1 -> x0, blocking collectives: 83.6 us -> none  [on_device(): lax.psum((first_term, second_term), ('gz', 'gy'))]
    ppermute x12 -> x0, starting transfers between devices: 46.5 us -> none  [the longest x6 36 us: extended(): lax.ppermute(tail, axis, [(i, (i + 1) % count) for i in range(ends)])]
    unnamed x93 -> x17, local copies, waits for them, and re-layouts: 39.9 us -> 3.13 us
    conv_general_dilated x14 -> x0, local copies, waits for them, and re-layouts: 32.4 us -> none  [convolve(): lax.conv_general_dilated(padded[None], kernel, (1, 1, 1), 'VALID', dimens...]
    conv_general_dilated x3 -> x0, matrix products: 30.1 us -> none  [convolve(): lax.conv_general_dilated(padded[None], kernel, (1, 1, 1), 'VALID', dimens...]
    all_to_all x2 -> x0, starting transfers between devices: 15.5 us -> none  [the longest x1 7.82 us: on_device(): lax.all_to_all(act_two.reshape(out_two, quart_d, quart_r * quart_w), 'gz'...]
  transfers between devices with their start and end apart: 15 -> 0, of which waited for: 2 -> 0; matrix products, arithmetic and copies ran while one was open for 18% -> 0% of each run, Pallas kernels for 0% -> 0%
where the time goes in v1:
time: 125 us; the launch traced here: 124 us
  Pallas kernels  104 us (83%)
  local copies, waits for them, and re-layouts  18.5 us (15%)
    pallas_call x5, Pallas kernels, kernel_call(): pl.pallas_call(body, out_shape=[jax.ShapeDtypeStruct(shape, dtype) for sh...  104 us
    unnamed x17, local copies, waits for them, and re-layouts  3.13 us

profile of v1, /device:TPU:1, one launch (start us, length us, event | category | flops | bytes accessed | tf_op | source)
XLA Modules:
  0.0 124.3 jit_solution(8982117177517868315)
XLA Ops:
  0.6 0.0 copy-start
  0.6 0.7 tile.5
  1.3 0.7 tile.4
  2.0 0.8 broadcast_in_dim_tile.8.b1_ref
  2.7 0.8 broadcast_in_dim_tile.9.b2_ref
  3.5 1.0 copy.17
  4.6 0.7 reshape.26.vol_ref
  5.2 0.9 reverse_bitcast_fusion
  6.2 24.9 %shard_map.112 = (bf16[10,96,256]{2,1,0:T(8,128)(2,1)}, bf16[64,256]{1,0:T(8,128)(2,1)}) custom-call(bf16[4,64,256]{2,1,0:T(8,128)(2,1)} %reshape.26.vol_ref, bf16[2,32,256]{2,1,0:T(8,128)(2,1)} %up_ref.1), custom_call_target="tpu_custom_call" | custom-call | tf_op jit(solution)/shard_map/pallas_call | solution.py:437
  31.1 0.8 bitcast_dynamic-update-slice_fusion.7
  31.8 0.8 bitcast_dynamic-update-slice_fusion.6
  32.6 0.0 copy-done
  32.9 0.6 copy.18
  33.5 0.4 reshape.27
  33.9 0.7 copy.20.w1_ref
  34.6 0.3 pad_bitcast_fusion.3
  34.9 0.4 pad_maximum_fusion.1
  35.3 0.8 copy.24
  36.1 0.0 copy-start.1
  36.1 1.9 %reshape.29.w3_ref = bf16[384,1024]{1,0:T(8,128)(2,1)} reshape(bf16[3,4,32,4,4,64]{5,4,3,2,1,0:T(4,128)(2,1)S(1)} %copy.24) | data formatting | bytes 1572864 | tf_op jit(solution)/shard_map/reshape | solution.py:465
  38.0 0.0 copy-done.1
  38.0 0.3 pad_bitcast_fusion.7
  38.3 0.4 pad_maximum_fusion
  38.7 1.2 copy.19
  39.9 1.0 reshape.28
  40.9 1.2 copy.22.w2_ref
  42.1 6.7 %shard_map.113 = (bf16[4,256,1280]{2,1,0:T(8,128)(2,1)}, bf16[4,256,1280]{2,1,0:T(8,128)(2,1)}, bf16[2,8,64,128]{3,2,1,0:T(8,128)(2,1)}, bf16[64,256]{1,0:T(8,128)(2,1)}, f32[512,128]{1,0:T(8,128)}) custom-call(bf16[10,96,256]{2,1,0:T(8,128)(2,1)} %get-tuple-element.13.ext_ref, bf16[64,256]{1,0:T(8,128)(2,1)} %get-tuple-element.14.back_ref, ...), custom_call_target="tpu_custom_call" | custom-call | tf_op jit(solution)/shard_map/pallas_call | solution.py:437
  48.8 38.6 %shard_map.114 = (bf16[4,10,64,128]{3,2,1,0:T(8,128)(2,1)}, bf16[2,32,256]{2,1,0:T(8,128)(2,1)}, f32[864,64]{1,0:T(8,128)}) custom-call(bf16[2,8,64,128]{3,2,1,0:T(8,128)(2,1)} %get-tuple-element.15.grad_ref, bf16[64,256]{1,0:T(8,128)(2,1)} %get-tuple-element.16.pool_ref, bf16[64,64]{1,0:T(8,128)(2,1)} %constant.10.clone.chan_ref, ...), custom_call_target="tpu_custom_call" | custom-call | tf_op jit(solution)/shard_map/pallas_call | solution.py:437
  87.4 0.0 copy-start.3
  87.4 0.0 copy-start.2
  87.4 5.5 %shard_map.115.term_ref = f32[32,128]{1,0:T(8,128)} custom-call(bf16[4,10,64,128]{3,2,1,0:T(8,128)(2,1)} %get-tuple-element.19.ext_ref, bf16[4,256,1280]{2,1,0:T(8,128)(2,1)} %get-tuple-element.20.patch_ref, bf16[4,256,1280]{2,1,0:T(8,128)(2,1)} %get-tuple-element.21.pre_ref, bf16[384,1024]{1,0:T(8,128)(2,1)} %reshape.29.w3_ref, ...), custom_call_target="tpu_custom_call" | custom-call | tf_op jit(solution)/shard_map/pallas_call | solution.py:437
  92.9 28.5 %shard_map.116 = f32[32,128]{1,0:T(8,128)} custom-call(f32[32,128]{1,0:T(8,128)} %shard_map.115.term_ref), custom_call_target="tpu_custom_call" | custom-call | tf_op jit(solution)/shard_map/pallas_call | solution.py:437
  121.4 0.7 slice_bitcast_fusion
  122.1 0.1 copy.25
  122.2 0.6 reshape.30
  122.9 0.0 copy-done.3
  122.9 0.6 copy.35
  123.5 0.0 copy-done.2
  123.5 0.8 copy.36
  (6 shorter events, 0.2 us)
Async XLA Ops:
  0.6 32.0 %copy-start = (bf16[3,3,3,4,32]{4,3,2,1,0:T(4,128)(2,1)S(1)}, bf16[3,3,3,4,32]{4,3,2,1,0:T(4,128)(2,1)}, u32[]{:S(2)}) copy-start(bf16[3,3,3,4,32]{4,3,2,1,0:T(4,128)(2,1)} %param.10) | copy-start | bytes 20740
  36.1 1.9 %copy-start.1 = (bf16[3,3,3,32,64]{4,3,2,1,0:T(8,128)(2,1)S(1)}, bf16[3,3,3,32,64]{4,3,2,1,0:T(8,128)(2,1)}, u32[]{:S(2)}) copy-start(bf16[3,3,3,32,64]{4,3,2,1,0:T(8,128)(2,1)} %param.12) | copy-start | bytes 331780
  87.4 35.5 %copy-start.3 = (bf16[2,32,256]{2,1,0:T(8,128)(2,1)S(1)}, bf16[2,32,256]{2,1,0:T(8,128)(2,1)}, u32[]{:S(2)}) copy-start(bf16[2,32,256]{2,1,0:T(8,128)(2,1)} %get-tuple-element.37) | copy-start | bytes 98308
  87.4 36.1 %copy-start.2 = (f32[864,64]{1,0:T(8,128)S(1)}, f32[864,64]{1,0:T(8,128)}, u32[]{:S(2)}) copy-start(f32[864,64]{1,0:T(8,128)} %get-tuple-element.22) | copy-start | bytes 663556

commit v2 on v0

v2 whole, which is shorter than its diff:
```python
import jax
import jax.numpy as jnp
import numpy as np
from jax import lax
from jax.experimental import pallas as pl
from jax.experimental.pallas import tpu as pltpu
from jax.sharding import PartitionSpec as P

LEAK = 0.3
F32 = jnp.float32
BF16 = jnp.bfloat16
MESH = pl.DeviceIdType.MESH
VMEM = pl.BlockSpec(memory_space=pltpu.VMEM)
GZ, GY = 32, 8
LIMIT = 56 * 2**20


def lanes_of(shape):
    return lax.broadcasted_iota(jnp.int32, shape, len(shape) - 1)


def before(x):
    lane = lanes_of(x.shape)
    return jnp.where(lane >= 64, pltpu.roll(x, 64, 1), jnp.where(lane == 0, 0.0, pltpu.roll(x, 65, 1)))


def after(x):
    lane = lanes_of(x.shape)
    return jnp.where(lane < 64, pltpu.roll(x, 64, 1), jnp.where(lane == 127, 0.0, pltpu.roll(x, 63, 1)))


def mm(a, b):
    return jnp.dot(a, b, preferred_element_type=F32)


def mm_nt(a, b):
    return lax.dot_general(a, b, (((1,), (1,)), ((), ())), preferred_element_type=F32)


def eye(n):
    return lax.broadcasted_iota(jnp.int32, (n, n), 0) == lax.broadcasted_iota(jnp.int32, (n, n), 1)


def one_hot(n):
    return jnp.where(eye(n), 1.0, 0.0).astype(BF16)


def column(row, times):
    n = row.shape[0]
    wide = jnp.broadcast_to(row[None, :], (n, n))
    once = jnp.sum(jnp.where(eye(n), wide, 0.0), axis=1, keepdims=True)
    return jnp.concatenate([once] * times, axis=0)


def place():
    return lax.axis_index("gz"), lax.axis_index("gy")


def spread_matrix():
    out = np.zeros((256, 4, 128), np.float32)
    for lane in range(128):
        cell = 2 * (lane % 64) + lane // 64
        for dw in range(4):
            w = 2 * cell + dw - 1
            if 0 <= w < 256:
                out[w, dw, lane] = 1
    return out.reshape(256, 512).astype(jnp.bfloat16)


def channel_matrix():
    out = np.zeros((64, 64), np.float32)
    for q in range(64):
        out[q, (q % 2) * 32 + q // 2] = 1
    return out.astype(jnp.bfloat16)


def turn_matrix():
    out = np.zeros((64, 64), np.float32)
    for r in range(16):
        for c in range(4):
            out[r * 4 + c, c * 16 + r] = 1
    return out.astype(jnp.bfloat16)


def gather_matrix():
    out = np.zeros((2, 2, 2, 4, 4, 4, 4, 128), np.float32)
    for pd in range(2):
        for pr in range(2):
            for pw in range(2):
                for r in range(3):
                    for s in range(3):
                        for t in range(3):
                            for c in range(4):
                                out[pd, pr, pw, pd + r, pw + t, pr + s, c, ((r * 3 + s) * 3 + t) * 4 + c] = 1
    return out.reshape(2048, 128).astype(jnp.bfloat16)


def around(dz, dy):
    gz, gy = place()
    return lax.rem(gz + dz + GZ, GZ), lax.rem(gy + dy + GY, GY)


def partner(kind, k):
    gz, gy = place()
    if kind == 0:
        return lax.rem(gz + 2 * k, GZ), gy
    if kind == 2:
        return lax.rem(gz + k, GZ), gy
    other = lax.rem(gy * 2 + lax.rem(gz, 2) + k, 16)
    return gz - lax.rem(gz, 2) + lax.rem(other, 2), other // 2


def rank(kind, gz, gy):
    return (gz // 2, gy * 2 + lax.rem(gz, 2), gz)[kind]


COUNT = (16, 16, 32)


def share(kind, source, landing, send, recv):
    gz, gy = place()
    slot = rank(kind, gz, gy)

    def go(k, _):
        to = partner(kind, k)
        pltpu.make_async_remote_copy(
            src_ref=source(rank(kind, *to)),
            dst_ref=landing.at[slot],
            send_sem=send,
            recv_sem=recv,
            device_id=to,
            device_id_type=MESH,
        ).start()
        return 0

    lax.fori_loop(1, COUNT[kind], go, 0)

    def wait():
        pltpu.make_async_remote_copy(
            src_ref=landing.at[pl.ds(0, COUNT[kind] - 1)],
            dst_ref=landing.at[pl.ds(0, COUNT[kind] - 1)],
            send_sem=send,
            recv_sem=recv,
            device_id=partner(kind, 1),
            device_id_type=MESH,
        ).wait()

    return wait


def greet():
    gz, gy = place()
    barrier = pltpu.get_barrier_semaphore()

    def tell(to):
        pl.semaphore_signal(barrier, inc=1, device_id=to, device_id_type=MESH)

    def along(k, _):
        tell((lax.rem(gz + k, GZ), gy))
        return 0

    def across(k, _):
        row = lax.rem(gy + k, GY)
        tell((gz, row))
        tell((gz + 1 - 2 * lax.rem(gz, 2), row))
        return 0

    far = lax.rem(gz + 2 * lax.rem(gz, 2) - 1 + GZ, GZ)
    tell((far, lax.rem(gy + 1, GY)))
    tell((far, lax.rem(gy + GY - 1, GY)))
    lax.fori_loop(1, GY, across, 0)
    lax.fori_loop(1, GZ, along, 0)

    def wait():
        pl.semaphore_wait(barrier, 47)

    return wait


def total16(landing):
    value = landing[0].astype(F32)
    for k in range(1, 16):
        value = value + landing[k].astype(F32)
    return value


def body(
    vol_ref, w1_ref, b1_ref, w2_ref, b2_ref, up_ref, spread_ref, chan_ref, turn_ref, gather_ref,
    pool_out, first_out, second_out,
    own, ext, up_stage, up_got, pool_stage, pool_got,
    w1_rows, w1, w2, w2_turned, rows, patch, pre, act, full, gact, ffull,
    sg, sg_one, sg_part, sg_two, sg_done, term, t_one, t_part, t_two,
    send, recv, a_send, a_recv, s_send, s_recv,
):
    gz, gy = place()
    greeted = greet()

    for d in range(4):
        flat = jnp.concatenate([vol_ref[c, d] for c in range(4)], axis=0)
        own[d] = mm(turn_ref[...], flat).astype(BF16)
    for half in range(2):
        for chan in range(2):
            up_stage[:, chan * 2 + half, :] = up_ref[chan, :, half * 128 : half * 128 + 128].astype(F32)
    w1_rows[...] = jnp.zeros((128, 32), F32)
    for i in range(27):
        w1_rows[4 * i : 4 * i + 4, :] = w1_ref[i // 9, i // 3 % 3, i % 3].astype(F32)
    flat = mm_nt(one_hot(32), w1_rows[...].astype(BF16)).astype(BF16)
    for g in range(8):
        w1[g * 32 : g * 32 + 32, :] = mm_nt(flat, gather_ref[g * 256 : g * 256 + 256, :]).astype(BF16)
    b1 = column(b1_ref[...], 8)
    b2 = column(b2_ref[...], 4)
    greeted()

    copies = []
    for dz in (-1, 1, 0):
        src_d, dst_d = {-1: (slice(0, 3), slice(7, 10)), 0: (slice(0, 4), slice(3, 7)), 1: (slice(1, 4), slice(0, 3))}[dz]
        for dy in (-1, 1, 0):
            if dz == 0 and dy == 0:
                continue
            src_r, dst_r = {
                -1: (slice(0, 16), slice(80, 96)),
                0: (slice(0, 64), slice(16, 80)),
                1: (slice(48, 64), slice(0, 16)),
            }[dy]
            copy = pltpu.make_async_remote_copy(
                src_ref=own.at[src_d, src_r],
                dst_ref=ext.at[dst_d, dst_r],
                send_sem=send.at[len(copies)],
                recv_sem=recv.at[len(copies)],
                device_id=around(dz, dy),
                device_id_type=MESH,
            )
            copy.start()
            copies.append(copy)
    up_wait = share(2, lambda j: up_stage.at[j], up_got, a_send.at[0], a_recv.at[0])

    lane = lanes_of((32, 128))
    zero = jnp.zeros((32, 128), F32)
    for t in range(3):
        for r in range(4):
            for s in range(4):
                at = ((r * 3 + t) * 4 + s) * 32
                for pd in range(2):
                    near = w2_ref[r - pd, s, t].astype(F32) if 0 <= r - pd < 3 and s < 3 else None
                    next_ = w2_ref[r - pd, s - 1, t].astype(F32) if 0 <= r - pd < 3 and s > 0 else None
                    left = zero[:, :64] if near is None else near
                    right = zero[:, :64] if next_ is None else next_
                    w2[at : at + 32, pd * 128 : pd * 128 + 128] = jnp.concatenate([left, right], axis=1).astype(BF16)
    w2_turned[...] = mm_nt(one_hot(256), w2[...]).astype(BF16)

    ext[3:7, 16:80] = own[...]
    for copy in copies:
        copy.wait()

    @pl.when(gz == 0)
    def _():
        ext[0:3] = jnp.zeros((3, 96, 256), BF16)

    @pl.when(gz == GZ - 1)
    def _():
        ext[7:10] = jnp.zeros((3, 96, 256), BF16)

    @pl.when(gy == 0)
    def _():
        ext[:, 0:16] = jnp.zeros((10, 16, 256), BF16)

    @pl.when(gy == GY - 1)
    def _():
        ext[:, 80:96] = jnp.zeros((10, 16, 256), BF16)

    def widen(d, _):
        wide = mm(ext[d], spread_ref[...])
        for dw in range(4):
            rows[d, dw] = wide[:, dw * 128 : dw * 128 + 128]
        return 0

    lax.fori_loop(0, 10, widen, 0)

    def inside(d, r):
        ok = jnp.where(d == 0, gz > 0, jnp.where(d == 3, gz < GZ - 1, True))
        if r == 0:
            ok = ok & (gy > 0)
        if r == 9:
            ok = ok & (gy < GY - 1)
        return ok

    def layer_one(d, _):
        for dd in range(4):
            for dw in range(4):
                for r in range(10):
                    patch[d, dd * 64 + dw * 16 : dd * 64 + dw * 16 + 16, r * 128 : r * 128 + 128] = rows[
                        2 * d + dd, dw, 8 * r + 4 : 8 * r + 20, :
                    ].astype(BF16)
        for j in range(5):
            value = mm(w1[...], patch[d, :, j * 256 : j * 256 + 256]) + b1
            pre[d, :, j * 256 : j * 256 + 256] = value.astype(BF16)
            out = jnp.maximum(value, LEAK * value)
            cell = out[0:32]
            for g in range(1, 8):
                cell = cell + out[g * 32 : g * 32 + 32]
            cell = (cell * 0.125).astype(BF16).astype(F32)
            for k in range(2):
                r = 2 * j + k
                one = jnp.where(inside(d, r), cell[:, k * 128 : k * 128 + 128], 0.0)
                act[d, 0, r * 32 : r * 32 + 32, :] = before(one).astype(BF16)
                act[d, 1, r * 32 : r * 32 + 32, :] = one.astype(BF16)
                act[d, 2, r * 32 : r * 32 + 32, :] = after(one).astype(BF16)
        return 0

    lax.fori_loop(0, 4, layer_one, 0)

    up_wait()
    up_got[gz] = up_stage[gz]
    lane = lanes_of((64, 128))
    wide = []
    for half in range(2):
        wide.append(jnp.concatenate([up_got[:, chan * 2 + half, :] for chan in range(2)], axis=0))
    back = mm(chan_ref[...], jnp.concatenate(wide, axis=1).astype(BF16))
    pooled = []
    grads = []
    for h in range(2):
        sides = []
        for k in range(2):
            r = 4 * h + 2 * k
            sides.append(
                jnp.concatenate([act[dd, dw, r * 32 : r * 32 + 128, :] for dd in range(4) for dw in range(3)], axis=0)
            )
        patches = jnp.concatenate(sides, axis=1)
        value = mm(w2_turned[...], patches) + b2
        out = jnp.maximum(value, LEAK * value)
        cell = out[0:64] + out[64:128] + out[128:192] + out[192:256]
        left, right = cell[:, :128], cell[:, 128:]
        left = left + pltpu.roll(left, 64, 1)
        right = right + pltpu.roll(right, 64, 1)
        pooled.append((jnp.where(lane < 64, left, right) * 0.125).astype(BF16))
        up = back[:, h * 128 : h * 128 + 128] * 0.125
        other = pltpu.roll(up, 64, 1)
        both = jnp.concatenate([jnp.where(lane < 64, up, other), jnp.where(lane < 64, other, up)], axis=1)
        weak = both * LEAK
        grad = jnp.concatenate(
            [jnp.where(value[g * 64 : g * 64 + 64] > 0, both, weak).astype(BF16) for g in range(4)], axis=0
        )
        grads.append(grad)
        if h == 0:
            full[...] = mm_nt(patches, grad)
        else:
            full[...] += mm_nt(patches, grad)

    lane = lanes_of((16, 128))
    for r in range(3):
        for t in range(3):
            near = []
            for s in range(4):
                a = ((r * 3 + t) * 4 + s) * 32
                b = (((r + 1) * 3 + t) * 4 + s) * 32
                near.append(full[a : a + 32, 0:128] + full[b : b + 32, 128:256])
            for s in range(3):
                low = near[s][:16] + pltpu.roll(near[s + 1][:16], 64, 1)
                high = pltpu.roll(near[s][16:], 64, 1) + near[s + 1][16:]
                at = (r * 3 + s) * 3 + t
                sg[at // 2, (at % 2) * 16 : (at % 2) * 16 + 16, :] = jnp.where(lane < 64, low, high).astype(SENT)
    sg[13, 16:32, :] = jnp.zeros((16, 128), SENT)
    sg[14:16] = jnp.zeros((2, 32, 128), SENT)
    chip, line = rank(0, gz, gy), rank(1, gz, gy)
    one_wait = share(0, lambda j: sg.at[j], sg_one, s_send.at[0], s_recv.at[0])
    sg_one[chip] = sg[chip]

    turned = lax.dot_general(
        chan_ref[...], jnp.concatenate(pooled, axis=1), (((0,), (0,)), ((), ())), preferred_element_type=F32
    )
    for half in range(2):
        for chan in range(2):
            pool_stage[:, chan * 2 + half, :] = turned[chan * 32 : chan * 32 + 32, half * 128 : half * 128 + 128]
    pool_wait = share(2, lambda j: pool_stage.at[j], pool_got, a_send.at[1], a_recv.at[1])
    pool_got[gz] = pool_stage[gz]

    for h in range(2):
        pulled = mm(w2[...], grads[h])
        for dd in range(4):
            for t in range(3):
                at = (dd * 3 + t) * 128
                for k in range(2):
                    gact[dd, t, 2 * h + k] = pulled[at : at + 128, k * 128 : k * 128 + 128]

    def layer_back(d, _):
        for j in range(5):
            sides = []
            for k in range(2):
                parts = []
                for t in range(3):
                    value = None
                    for r, at in ((j, k * 32), (j - 1, 64 + k * 32)):
                        if 0 <= r < 4:
                            piece = gact[d, t, r, at : at + 32, :]
                            value = piece if value is None else value + piece
                    parts.append(value)
                value = (after(parts[0]) + parts[1] + before(parts[2])) * 0.125
                sides.append(jnp.where(inside(d, 2 * j + k), value, 0.0))
            strong = jnp.concatenate(sides, axis=1)
            weak = strong * LEAK
            seen = pre[d, :, j * 256 : j * 256 + 256].astype(F32)
            grad = jnp.concatenate(
                [jnp.where(seen[g * 32 : g * 32 + 32] > 0, strong, weak).astype(BF16) for g in range(8)], axis=0
            )
            ffull[...] += mm_nt(grad, patch[d, :, j * 256 : j * 256 + 256])
        return 0

    ffull[...] = jnp.zeros((256, 256), F32)
    lax.fori_loop(0, 4, layer_back, 0)
    flat = jnp.concatenate([ffull[g * 32 : g * 32 + 32, :] for g in range(8)], axis=1)
    total = jnp.zeros((32, 128), F32)
    for _ in range(3):
        piece = flat.astype(BF16)
        total = total + mm(piece, gather_ref[...])
        flat = flat - piece.astype(F32)
    term[...] = total.astype(SENT)

    t_wait = share(0, lambda j: term, t_one, s_send.at[3], s_recv.at[3])
    t_one[chip] = term[...]
    one_wait()
    sg_part[...] = total16(sg_one).astype(SENT)
    two_wait = share(1, lambda j: sg_part, sg_two, s_send.at[1], s_recv.at[1])
    sg_two[line] = sg_part[...]
    t_wait()
    t_part[...] = total16(t_one).astype(SENT)
    t_wait = share(1, lambda j: t_part, t_two, s_send.at[4], s_recv.at[4])
    t_two[line] = t_part[...]
    two_wait()
    sg_done[chip] = total16(sg_two).astype(SENT)
    done_wait = share(0, lambda j: sg_done.at[chip], sg_done, s_send.at[2], s_recv.at[2])
    pool_wait()
    for half in range(2):
        for chan in range(2):
            pool_out[chan, :, half * 128 : half * 128 + 128] = pool_got[:, chan * 2 + half, :].astype(BF16)
    t_wait()
    turned = jnp.transpose(total16(t_two))
    for i in range(27):
        first_out[i // 9, i // 3 % 3, i % 3] = turned[4 * i : 4 * i + 4, :]
    done_wait()
    for i in range(27):
        block = sg_done[i // 2, (i % 2) * 16 : (i % 2) * 16 + 16, :].astype(F32)
        second_out[i // 9, i // 3 % 3, i % 3, 0:16, :] = block[:, :64]
        second_out[i // 9, i // 3 % 3, i % 3, 16:32, :] = block[:, 64:]


SENT = F32


def on_device(volume, first_weight, first_bias, second_weight, second_bias, upstream):
    dma, mem = pltpu.SemaphoreType.DMA, pltpu.VMEM
    constants = [jnp.asarray(m()) for m in (spread_matrix, channel_matrix, turn_matrix, gather_matrix)]
    operands = [volume, first_weight, first_bias, second_weight, second_bias, upstream, *constants]
    return pl.pallas_call(
        body,
        out_shape=[
            jax.ShapeDtypeStruct((2, 32, 256), BF16),
            jax.ShapeDtypeStruct((3, 3, 3, 4, 32), F32),
            jax.ShapeDtypeStruct((3, 3, 3, 32, 64), F32),
        ],
        in_specs=[VMEM] * len(operands),
        out_specs=[VMEM] * 3,
        scratch_shapes=[
            mem((4, 64, 256), BF16), mem((10, 96, 256), BF16), mem((32, 8, 128), F32), mem((32, 8, 128), F32),
            mem((32, 8, 128), F32), mem((32, 8, 128), F32),
            mem((128, 32), F32), mem((256, 256), BF16), mem((1536, 256), BF16), mem((256, 1536), BF16),
            mem((10, 4, 96, 128), F32), mem((4, 256, 1280), BF16), mem((4, 256, 1280), BF16), mem((4, 3, 320, 128), BF16),
            mem((1536, 256), F32), mem((4, 3, 4, 128, 128), F32), mem((256, 256), F32),
            mem((16, 32, 128), SENT), mem((16, 32, 128), SENT), mem((32, 128), SENT), mem((16, 32, 128), SENT),
            mem((16, 32, 128), SENT), mem((32, 128), SENT), mem((16, 32, 128), SENT), mem((32, 128), SENT),
            mem((16, 32, 128), SENT),
            dma((8,)), dma((8,)), dma((2,)), dma((2,)), dma((5,)), dma((5,)),
        ],
        compiler_params=pltpu.CompilerParams(vmem_limit_bytes=LIMIT, has_side_effects=True, collective_id=1),
    )(*operands)


def solution(mesh):
    placed = (P(None, "gz", "gy", None), P(), P(), P(), P(), P("gz", None, "gy"))
    return jax.shard_map(
        on_device,
        mesh=mesh,
        in_specs=placed,
        out_specs=(P("gz", None, "gy"), P(), P()),
        check_vma=False,
    )
```

time: 494 us -> 50 us (0.10); the launches traced: 484 us -> 49.8 us
  waiting for transfers between devices: 153 us -> 0 us
  local copies, waits for them, and re-layouts: 101 us -> 3.82 us
  blocking collectives: 83.6 us -> 0 us
  starting transfers between devices: 62 us -> 0 us
  Pallas kernels: 0 us -> 45.4 us
  matrix products: 36.4 us -> 0 us
  other arithmetic: 32.8 us -> 0 us
  between operations: 15.3 us -> 0.65 us
    psum x1 -> x0, waiting for transfers between devices: 152 us -> none  [on_device(): lax.psum((first_term, second_term), ('gz', 'gy'))]
    psum x1 -> x0, blocking collectives: 83.6 us -> none  [on_device(): lax.psum((first_term, second_term), ('gz', 'gy'))]
    ppermute x12 -> x0, starting transfers between devices: 46.5 us -> none  [the longest x6 36 us: extended(): lax.ppermute(tail, axis, [(i, (i + 1) % count) for i in range(ends)])]
    pallas_call x0 -> x1, Pallas kernels: none -> 45.4 us  [on_device(): pl.pallas_call(body, out_shape=[jax.ShapeDtypeStruct((2, 32, 256), BF16),...]
    unnamed x93 -> x5, local copies, waits for them, and re-layouts: 39.9 us -> 3.82 us
    conv_general_dilated x14 -> x0, local copies, waits for them, and re-layouts: 32.4 us -> none  [convolve(): lax.conv_general_dilated(padded[None], kernel, (1, 1, 1), 'VALID', dimens...]
    conv_general_dilated x3 -> x0, matrix products: 30.1 us -> none  [convolve(): lax.conv_general_dilated(padded[None], kernel, (1, 1, 1), 'VALID', dimens...]
    all_to_all x2 -> x0, starting transfers between devices: 15.5 us -> none  [the longest x1 7.82 us: on_device(): lax.all_to_all(act_two.reshape(out_two, quart_d, quart_r * quart_w), 'gz'...]
  transfers between devices with their start and end apart: 15 -> 0, of which waited for: 2 -> 0; matrix products, arithmetic and copies ran while one was open for 18% -> 0% of each run, Pallas kernels for 0% -> 0%
where the time goes in v2:
time: 50 us; the launch traced here: 49.8 us
  Pallas kernels  45.4 us (91%)
  local copies, waits for them, and re-layouts  3.82 us (8%)
  between operations  0.65 us (1%)
    pallas_call x1, Pallas kernels, on_device(): pl.pallas_call(body, out_shape=[jax.ShapeDtypeStruct((2, 32, 256), BF16),...  45.4 us
    unnamed x5, local copies, waits for them, and re-layouts  3.82 us

profile of v2, /device:TPU:1, one launch (start us, length us, event | category | flops | bytes accessed | tf_op | source)
XLA Modules:
  0.0 49.8 jit_solution(13929467029477679062)
XLA Ops:
  0.6 45.4 %shard_map.121 = (bf16[2,32,256]{2,1,0:T(8,128)(2,1)}, f32[3,3,3,4,32]{4,3,2,1,0:T(4,128)}, f32[3,3,3,32,64]{4,3,2,1,0:T(8,128)}) custom-call(bf16[4,4,16,256]{3,2,1,0:T(8,128)(2,1)} %vol_ref.1, bf16[3,3,3,4,32]{4,3,2,1,0:T(4,128)(2,1)} %w1_ref.1, f32[32]{0:T(128)} %b1_ref.1, bf16[3,3,3,32,64]{4,3,2,1,0:T(8,128)(2,1)} %w2_ref.1, f32[64]{0:T(128)} %b2_ref.1, ...), custom_call_target="tpu_custom_call" | custom-call | tf_op jit(solution)/shard_map/pallas_call | solution.py:453
  46.0 0.0 copy-start
  46.0 1.4 %copy.16 = bf16[2,32,256]{2,1,0:T(8,128)(2,1)} copy(bf16[2,32,256]{2,1,0:T(8,128)(2,1)} %get-tuple-element.6) | data formatting | bytes 65536
  47.4 0.0 copy-done
  47.4 0.6 %copy.17 = f32[3,3,3,4,32]{4,3,2,1,0:T(4,128)} copy(f32[3,3,3,4,32]{4,3,2,1,0:T(4,128)S(1)} %copy-done) | data formatting | bytes 27648
  48.0 1.8 %copy.18 = f32[3,3,3,32,64]{4,3,2,1,0:T(8,128)} copy(f32[3,3,3,32,64]{4,3,2,1,0:T(8,128)} %get-tuple-element.8) | data formatting | bytes 442368
Async XLA Ops:
  46.0 1.4 %copy-start = (f32[3,3,3,4,32]{4,3,2,1,0:T(4,128)S(1)}, f32[3,3,3,4,32]{4,3,2,1,0:T(4,128)}, u32[]{:S(2)}) copy-start(f32[3,3,3,4,32]{4,3,2,1,0:T(4,128)} %get-tuple-element.7) | copy-start | bytes 41476

commit v3 on v2

--- a/solution.py
+++ b/solution.py
@@ -100,14 +100,21 @@
     return lax.rem(gz + dz + GZ, GZ), lax.rem(gy + dy + GY, GY)
 
 
-def partner(kind, k):
+def spread_order(kind):
+    xs, ys, zs, cores = (range(n) for n in ((4, 4, 1, 1), (1, 1, 8, 2), (4, 4, 1, 2))[kind])
+    all_ = [(x, y, z, c) for x in xs for y in ys for z in zs for c in cores]
+    hops = lambda o: min(o[0], 4 - o[0]) + min(o[1], 4 - o[1]) + min(o[2], 8 - o[2]) + 0.5 * o[3]
+    return sorted([o for o in all_ if any(o)], key=lambda o: -hops(o))
+
+
+def shifted(offset):
     gz, gy = place()
-    if kind == 0:
-        return lax.rem(gz + 2 * k, GZ), gy
-    if kind == 2:
-        return lax.rem(gz + k, GZ), gy
-    other = lax.rem(gy * 2 + lax.rem(gz, 2) + k, 16)
-    return gz - lax.rem(gz, 2) + lax.rem(other, 2), other // 2
+    x, y, core = gz // 8, lax.rem(gz // 2, 4), lax.rem(gz, 2)
+    dx, dy, dz, dc = offset
+    x = lax.rem(x + dx, 4) if dx else x
+    y = lax.rem(y + dy, 4) if dy else y
+    core = 1 - core if dc else core
+    return x * 8 + y * 2 + core, lax.rem(gy + dz, GY) if dz else gy
 
 
 def rank(kind, gz, gy):
@@ -120,9 +127,8 @@
 def share(kind, source, landing, send, recv):
     gz, gy = place()
     slot = rank(kind, gz, gy)
-
-    def go(k, _):
-        to = partner(kind, k)
+    for offset in spread_order(kind):
+        to = shifted(offset)
         pltpu.make_async_remote_copy(
             src_ref=source(rank(kind, *to)),
             dst_ref=landing.at[slot],
@@ -131,9 +137,6 @@
             device_id=to,
             device_id_type=MESH,
         ).start()
-        return 0
-
-    lax.fori_loop(1, COUNT[kind], go, 0)
 
     def wait():
         pltpu.make_async_remote_copy(
@@ -141,7 +144,7 @@
             dst_ref=landing.at[pl.ds(0, COUNT[kind] - 1)],
             send_sem=send,
             recv_sem=recv,
-            device_id=partner(kind, 1),
+            device_id=around(1, 0),
             device_id_type=MESH,
         ).wait()
 
@@ -155,21 +158,14 @@
     def tell(to):
         pl.semaphore_signal(barrier, inc=1, device_id=to, device_id_type=MESH)
 
-    def along(k, _):
-        tell((lax.rem(gz + k, GZ), gy))
-        return 0
-
-    def across(k, _):
-        row = lax.rem(gy + k, GY)
-        tell((gz, row))
-        tell((gz + 1 - 2 * lax.rem(gz, 2), row))
-        return 0
-
     far = lax.rem(gz + 2 * lax.rem(gz, 2) - 1 + GZ, GZ)
+    for offset in spread_order(1):
+        if offset[2]:
+            tell(shifted(offset))
+    for offset in spread_order(2):
+        tell(shifted(offset))
     tell((far, lax.rem(gy + 1, GY)))
     tell((far, lax.rem(gy + GY - 1, GY)))
-    lax.fori_loop(1, GY, across, 0)
-    lax.fori_loop(1, GZ, along, 0)
 
     def wait():
         pl.semaphore_wait(barrier, 47)
@@ -433,35 +429,40 @@
         for chan in range(2):
             pool_out[chan, :, half * 128 : half * 128 + 128] = pool_got[:, chan * 2 + half, :].astype(BF16)
     t_wait()
-    turned = jnp.transpose(total16(t_two))
+    first_out[...] = total16(t_two)
+    done_wait()
+    second_out[...] = sg_done[...]
+
+
+def finish(pool_in, first_in, second_in, pool_out, first_out, second_out):
+    pool_out[...] = pool_in[...]
+    turned = jnp.transpose(first_in[...])
     for i in range(27):
         first_out[i // 9, i // 3 % 3, i % 3] = turned[4 * i : 4 * i + 4, :]
-    done_wait()
-    for i in range(27):
-        block = sg_done[i // 2, (i % 2) * 16 : (i % 2) * 16 + 16, :].astype(F32)
+        block = second_in[i // 2, (i % 2) * 16 : (i % 2) * 16 + 16, :].astype(F32)
         second_out[i // 9, i // 3 % 3, i % 3, 0:16, :] = block[:, :64]
         second_out[i // 9, i // 3 % 3, i % 3, 16:32, :] = block[:, 64:]
 
 
-SENT = F32
+SENT = BF16
 
 
 def on_device(volume, first_weight, first_bias, second_weight, second_bias, upstream):
     dma, mem = pltpu.SemaphoreType.DMA, pltpu.VMEM
     constants = [jnp.asarray(m()) for m in (spread_matrix, channel_matrix, turn_matrix, gather_matrix)]
     operands = [volume, first_weight, first_bias, second_weight, second_bias, upstream, *constants]
-    return pl.pallas_call(
+    results = pl.pallas_call(
         body,
         out_shape=[
             jax.ShapeDtypeStruct((2, 32, 256), BF16),
-            jax.ShapeDtypeStruct((3, 3, 3, 4, 32), F32),
-            jax.ShapeDtypeStruct((3, 3, 3, 32, 64), F32),
+            jax.ShapeDtypeStruct((32, 128), F32),
+            jax.ShapeDtypeStruct((16, 32, 128), SENT),
         ],
         in_specs=[VMEM] * len(operands),
         out_specs=[VMEM] * 3,
         scratch_shapes=[
-            mem((4, 64, 256), BF16), mem((10, 96, 256), BF16), mem((32, 8, 128), F32), mem((32, 8, 128), F32),
-            mem((32, 8, 128), F32), mem((32, 8, 128), F32),
+            mem((4, 64, 256), BF16), mem((10, 96, 256), BF16), mem((32, 4, 128), F32), mem((32, 4, 128), F32),
+            mem((32, 4, 128), F32), mem((32, 4, 128), F32),
             mem((128, 32), F32), mem((256, 256), BF16), mem((1536, 256), BF16), mem((256, 1536), BF16),
             mem((10, 4, 96, 128), F32), mem((4, 256, 1280), BF16), mem((4, 256, 1280), BF16), mem((4, 3, 320, 128), BF16),
             mem((1536, 256), F32), mem((4, 3, 4, 128, 128), F32), mem((256, 256), F32),
@@ -472,6 +473,16 @@
         ],
         compiler_params=pltpu.CompilerParams(vmem_limit_bytes=LIMIT, has_side_effects=True, collective_id=1),
     )(*operands)
+    return pl.pallas_call(
+        finish,
+        out_shape=[
+            jax.ShapeDtypeStruct((2, 32, 256), BF16),
+            jax.ShapeDtypeStruct((3, 3, 3, 4, 32), F32),
+            jax.ShapeDtypeStruct((3, 3, 3, 32, 64), F32),
+        ],
+        in_specs=[VMEM] * 3,
+        out_specs=[VMEM] * 3,
+    )(*results)
 
 
 def solution(mesh):

time: 50 us -> 40 us (0.80)
  Pallas kernels: 45.4 us -> 39.2 us
  local copies, waits for them, and re-layouts: 3.82 us -> 0 us
    pallas_call x1, Pallas kernels: 45.4 us -> 37.4 us  [on_device(): pl.pallas_call(body, out_shape=[jax.ShapeDtypeStruct((2, 32, 256), BF16),...]
    unnamed x5 -> x0, local copies, waits for them, and re-layouts: 3.82 us -> none
    pallas_call x0 -> x1, Pallas kernels: none -> 1.83 us  [on_device(): pl.pallas_call(finish, out_shape=[jax.ShapeDtypeStruct((2, 32, 256), BF16...]
where the time goes in v3:
time: 40 us; the launch traced here: 39.9 us
  Pallas kernels  39.2 us (98%)
  between operations  0.64 us (2%)
    pallas_call x1, Pallas kernels, on_device(): pl.pallas_call(body, out_shape=[jax.ShapeDtypeStruct((2, 32, 256), BF16),...  37.4 us
    pallas_call x1, Pallas kernels, on_device(): pl.pallas_call(finish, out_shape=[jax.ShapeDtypeStruct((2, 32, 256), BF16...  1.83 us

profile of v3, /device:TPU:1, one launch (start us, length us, event | category | flops | bytes accessed | tf_op | source)
XLA Modules:
  0.0 39.9 jit_solution(17728649273197022518)
XLA Ops:
  0.6 37.4 %shard_map.121 = (bf16[2,32,256]{2,1,0:T(8,128)(2,1)}, f32[32,128]{1,0:T(8,128)}, bf16[16,32,128]{2,1,0:T(8,128)(2,1)}) custom-call(bf16[4,4,16,256]{3,2,1,0:T(8,128)(2,1)} %vol_ref.1, bf16[3,3,3,4,32]{4,3,2,1,0:T(4,128)(2,1)} %w1_ref.1, f32[32]{0:T(128)} %b1_ref.1, bf16[3,3,3,32,64]{4,3,2,1,0:T(8,128)(2,1)} %w2_ref.1, f32[64]{0:T(128)} %b2_ref.1, ...), custom_call_target="tpu_custom_call" | custom-call | tf_op jit(solution)/shard_map/pallas_call | solution.py:454
  38.0 1.8 %shard_map.122 = (bf16[2,32,256]{2,1,0:T(8,128)(2,1)}, f32[3,3,3,4,32]{4,3,2,1,0:T(4,128)}, f32[3,3,3,32,64]{4,3,2,1,0:T(8,128)}) custom-call(bf16[2,32,256]{2,1,0:T(8,128)(2,1)} %get-tuple-element.6.pool_in, f32[32,128]{1,0:T(8,128)} %get-tuple-element.7.first_in, bf16[16,32,128]{2,1,0:T(8,128)(2,1)} %get-tuple-element.8.second_in), custom_call_target="tpu_custom_call" | custom-call | tf_op jit(solution)/shard_map/pallas_call | solution.py:476

commit v4 on v3

--- a/solution.py
+++ b/solution.py
@@ -264,13 +264,11 @@
     def _():
         ext[:, 80:96] = jnp.zeros((10, 16, 256), BF16)
 
-    def widen(d, _):
-        wide = mm(ext[d], spread_ref[...])
-        for dw in range(4):
-            rows[d, dw] = wide[:, dw * 128 : dw * 128 + 128]
-        return 0
-
-    lax.fori_loop(0, 10, widen, 0)
+    flat = ext[...].reshape(960, 256)
+    for side in range(2):
+        wide = mm(flat, spread_ref[:, side * 256 : side * 256 + 256])
+        for k in range(2):
+            rows[:, 2 * side + k] = wide[:, k * 128 : k * 128 + 128].reshape(10, 96, 128)
 
     def inside(d, r):
         ok = jnp.where(d == 0, gz > 0, jnp.where(d == 3, gz < GZ - 1, True))
@@ -303,7 +301,7 @@
                 act[d, 2, r * 32 : r * 32 + 32, :] = after(one).astype(BF16)
         return 0
 
-    lax.fori_loop(0, 4, layer_one, 0)
+    lax.fori_loop(0, 4, layer_one, 0, unroll=True)
 
     up_wait()
     up_got[gz] = up_stage[gz]
@@ -367,8 +365,6 @@
     for half in range(2):
         for chan in range(2):
             pool_stage[:, chan * 2 + half, :] = turned[chan * 32 : chan * 32 + 32, half * 128 : half * 128 + 128]
-    pool_wait = share(2, lambda j: pool_stage.at[j], pool_got, a_send.at[1], a_recv.at[1])
-    pool_got[gz] = pool_stage[gz]
 
     for h in range(2):
         pulled = mm(w2[...], grads[h])
@@ -402,13 +398,14 @@
         return 0
 
     ffull[...] = jnp.zeros((256, 256), F32)
-    lax.fori_loop(0, 4, layer_back, 0)
+    lax.fori_loop(0, 4, layer_back, 0, unroll=True)
     flat = jnp.concatenate([ffull[g * 32 : g * 32 + 32, :] for g in range(8)], axis=1)
-    total = jnp.zeros((32, 128), F32)
+    pieces = []
     for _ in range(3):
-        piece = flat.astype(BF16)
-        total = total + mm(piece, gather_ref[...])
-        flat = flat - piece.astype(F32)
+        pieces.append(flat.astype(BF16))
+        flat = flat - pieces[-1].astype(F32)
+    total = mm(jnp.concatenate(pieces, axis=0), gather_ref[...])
+    total = total[0:32] + total[32:64] + total[64:96]
     term[...] = total.astype(SENT)
 
     t_wait = share(0, lambda j: term, t_one, s_send.at[3], s_recv.at[3])
@@ -416,6 +413,8 @@
     one_wait()
     sg_part[...] = total16(sg_one).astype(SENT)
     two_wait = share(1, lambda j: sg_part, sg_two, s_send.at[1], s_recv.at[1])
+    pool_wait = share(2, lambda j: pool_stage.at[j], pool_got, a_send.at[1], a_recv.at[1])
+    pool_got[gz] = pool_stage[gz]
     sg_two[line] = sg_part[...]
     t_wait()
     t_part[...] = total16(t_one).astype(SENT)

time: 40 us -> 39 us (0.975)
  Pallas kernels: 39.2 us -> 38.2 us
    pallas_call x1, Pallas kernels: 37.4 us -> 36.4 us  [on_device(): pl.pallas_call(body, out_shape=[jax.ShapeDtypeStruct((2, 32, 256), BF16),...]
where the time goes in v4:
time: 39 us; the launch traced here: 38.9 us
  Pallas kernels  38.2 us (98%)
  between operations  0.64 us (2%)
    pallas_call x1, Pallas kernels, on_device(): pl.pallas_call(body, out_shape=[jax.ShapeDtypeStruct((2, 32, 256), BF16),...  36.4 us
    pallas_call x1, Pallas kernels, on_device(): pl.pallas_call(finish, out_shape=[jax.ShapeDtypeStruct((2, 32, 256), BF16...  1.83 us

profile of v4, /device:TPU:1, one launch (start us, length us, event | category | flops | bytes accessed | tf_op | source)
XLA Modules:
  0.0 38.9 jit_solution(1366772458853011992)
XLA Ops:
  0.6 36.4 %shard_map.121 = (bf16[2,32,256]{2,1,0:T(8,128)(2,1)}, f32[32,128]{1,0:T(8,128)}, bf16[16,32,128]{2,1,0:T(8,128)(2,1)}) custom-call(bf16[4,4,16,256]{3,2,1,0:T(8,128)(2,1)} %vol_ref.1, bf16[3,3,3,4,32]{4,3,2,1,0:T(4,128)(2,1)} %w1_ref.1, f32[32]{0:T(128)} %b1_ref.1, bf16[3,3,3,32,64]{4,3,2,1,0:T(8,128)(2,1)} %w2_ref.1, f32[64]{0:T(128)} %b2_ref.1, ...), custom_call_target="tpu_custom_call" | custom-call | tf_op jit(solution)/shard_map/pallas_call | solution.py:453
  37.0 1.8 %shard_map.122 = (bf16[2,32,256]{2,1,0:T(8,128)(2,1)}, f32[3,3,3,4,32]{4,3,2,1,0:T(4,128)}, f32[3,3,3,32,64]{4,3,2,1,0:T(8,128)}) custom-call(bf16[2,32,256]{2,1,0:T(8,128)(2,1)} %get-tuple-element.6.pool_in, f32[32,128]{1,0:T(8,128)} %get-tuple-element.7.first_in, bf16[16,32,128]{2,1,0:T(8,128)(2,1)} %get-tuple-element.8.second_in), custom_call_target="tpu_custom_call" | custom-call | tf_op jit(solution)/shard_map/pallas_call | solution.py:475

commit v5 on v4

--- a/solution.py
+++ b/solution.py
@@ -124,10 +124,12 @@
 COUNT = (16, 16, 32)
 
 
-def share(kind, source, landing, send, recv):
+def share(kind, source, landing, send, recv, after=0, then=None):
     gz, gy = place()
     slot = rank(kind, gz, gy)
-    for offset in spread_order(kind):
+    for number, offset in enumerate(spread_order(kind)):
+        if then is not None and number == after:
+            then()
         to = shifted(offset)
         pltpu.make_async_remote_copy(
             src_ref=source(rank(kind, *to)),
@@ -181,15 +183,28 @@
 
 
 def body(
-    vol_ref, w1_ref, b1_ref, w2_ref, b2_ref, up_ref, spread_ref, chan_ref, turn_ref, gather_ref,
+    vol_in, w1_in, b1_in, w2_in, b2_in, up_in, spread_in, chan_in, turn_in, gather_in,
     pool_out, first_out, second_out,
+    vol_ref, w1_ref, b1_ref, w2_ref, b2_ref, up_ref, spread_ref, chan_ref, turn_ref, gather_ref, load, seen,
     own, ext, up_stage, up_got, pool_stage, pool_got,
     w1_rows, w1, w2, w2_turned, rows, patch, pre, act, full, gact, ffull,
     sg, sg_one, sg_part, sg_two, sg_done, term, t_one, t_part, t_two,
     send, recv, a_send, a_recv, s_send, s_recv,
 ):
     gz, gy = place()
+    loads = []
+    for source, target in (
+        (vol_in, vol_ref), (turn_in, turn_ref), (up_in, up_ref), (w1_in, w1_ref), (gather_in, gather_ref),
+        (b1_in, b1_ref), (b2_in, b2_ref), (w2_in, w2_ref), (spread_in, spread_ref), (chan_in, chan_ref),
+    ):
+        loads.append(pltpu.make_async_copy(source, target, load.at[len(loads)]))
+    for one in loads[:3]:
+        one.start()
     greeted = greet()
+    for one in loads[3:]:
+        one.start()
+    for one in loads[:3]:
+        one.wait()
 
     for d in range(4):
         flat = jnp.concatenate([vol_ref[c, d] for c in range(4)], axis=0)
@@ -197,6 +212,8 @@
     for half in range(2):
         for chan in range(2):
             up_stage[:, chan * 2 + half, :] = up_ref[chan, :, half * 128 : half * 128 + 128].astype(F32)
+    for one in loads[3:7]:
+        one.wait()
     w1_rows[...] = jnp.zeros((128, 32), F32)
     for i in range(27):
         w1_rows[4 * i : 4 * i + 4, :] = w1_ref[i // 9, i // 3 % 3, i % 3].astype(F32)
@@ -208,27 +225,32 @@
     greeted()
 
     copies = []
-    for dz in (-1, 1, 0):
-        src_d, dst_d = {-1: (slice(0, 3), slice(7, 10)), 0: (slice(0, 4), slice(3, 7)), 1: (slice(1, 4), slice(0, 3))}[dz]
-        for dy in (-1, 1, 0):
-            if dz == 0 and dy == 0:
-                continue
-            src_r, dst_r = {
-                -1: (slice(0, 16), slice(80, 96)),
-                0: (slice(0, 64), slice(16, 80)),
-                1: (slice(48, 64), slice(0, 16)),
-            }[dy]
-            copy = pltpu.make_async_remote_copy(
-                src_ref=own.at[src_d, src_r],
-                dst_ref=ext.at[dst_d, dst_r],
-                send_sem=send.at[len(copies)],
-                recv_sem=recv.at[len(copies)],
-                device_id=around(dz, dy),
-                device_id_type=MESH,
-            )
-            copy.start()
-            copies.append(copy)
-    up_wait = share(2, lambda j: up_stage.at[j], up_got, a_send.at[0], a_recv.at[0])
+
+    def send_halo():
+        for dz in (-1, 1, 0):
+            src_d, dst_d = {-1: (slice(0, 3), slice(7, 10)), 0: (slice(0, 4), slice(3, 7)), 1: (slice(1, 4), slice(0, 3))}[dz]
+            for dy in (-1, 1, 0):
+                if dz == 0 and dy == 0:
+                    continue
+                src_r, dst_r = {
+                    -1: (slice(0, 16), slice(80, 96)),
+                    0: (slice(0, 64), slice(16, 80)),
+                    1: (slice(48, 64), slice(0, 16)),
+                }[dy]
+                copy = pltpu.make_async_remote_copy(
+                    src_ref=own.at[src_d, src_r],
+                    dst_ref=ext.at[dst_d, dst_r],
+                    send_sem=send.at[len(copies)],
+                    recv_sem=recv.at[len(copies)],
+                    device_id=around(dz, dy),
+                    device_id_type=MESH,
+                )
+                copy.start()
+                copies.append(copy)
+
+    up_wait = share(2, lambda j: up_stage.at[j], up_got, a_send.at[0], a_recv.at[0], 10, send_halo)
+    for one in loads[7:]:
+        one.wait()
 
     lane = lanes_of((32, 128))
     zero = jnp.zeros((32, 128), F32)
@@ -303,42 +325,54 @@
 
     lax.fori_loop(0, 4, layer_one, 0, unroll=True)
 
-    up_wait()
-    up_got[gz] = up_stage[gz]
     lane = lanes_of((64, 128))
-    wide = []
-    for half in range(2):
-        wide.append(jnp.concatenate([up_got[:, chan * 2 + half, :] for chan in range(2)], axis=0))
-    back = mm(chan_ref[...], jnp.concatenate(wide, axis=1).astype(BF16))
     pooled = []
-    grads = []
-    for h in range(2):
+
+    def windows(h):
         sides = []
         for k in range(2):
             r = 4 * h + 2 * k
             sides.append(
                 jnp.concatenate([act[dd, dw, r * 32 : r * 32 + 128, :] for dd in range(4) for dw in range(3)], axis=0)
             )
-        patches = jnp.concatenate(sides, axis=1)
-        value = mm(w2_turned[...], patches) + b2
+        return jnp.concatenate(sides, axis=1)
+
+    for h in range(2):
+        value = mm(w2_turned[...], windows(h)) + b2
+        seen[h] = value
         out = jnp.maximum(value, LEAK * value)
         cell = out[0:64] + out[64:128] + out[128:192] + out[192:256]
         left, right = cell[:, :128], cell[:, 128:]
         left = left + pltpu.roll(left, 64, 1)
         right = right + pltpu.roll(right, 64, 1)
         pooled.append((jnp.where(lane < 64, left, right) * 0.125).astype(BF16))
+    turned = lax.dot_general(
+        chan_ref[...], jnp.concatenate(pooled, axis=1), (((0,), (0,)), ((), ())), preferred_element_type=F32
+    )
+    for half in range(2):
+        for chan in range(2):
+            pool_stage[:, chan * 2 + half, :] = turned[chan * 32 : chan * 32 + 32, half * 128 : half * 128 + 128]
+
+    up_wait()
+    up_got[gz] = up_stage[gz]
+    wide = []
+    for half in range(2):
+        wide.append(jnp.concatenate([up_got[:, chan * 2 + half, :] for chan in range(2)], axis=0))
+    back = mm(chan_ref[...], jnp.concatenate(wide, axis=1).astype(BF16))
+    grads = []
+    for h in range(2):
         up = back[:, h * 128 : h * 128 + 128] * 0.125
         other = pltpu.roll(up, 64, 1)
         both = jnp.concatenate([jnp.where(lane < 64, up, other), jnp.where(lane < 64, other, up)], axis=1)
         weak = both * LEAK
         grad = jnp.concatenate(
-            [jnp.where(value[g * 64 : g * 64 + 64] > 0, both, weak).astype(BF16) for g in range(4)], axis=0
+            [jnp.where(seen[h, g * 64 : g * 64 + 64] > 0, both, weak).astype(BF16) for g in range(4)], axis=0
         )
         grads.append(grad)
         if h == 0:
-            full[...] = mm_nt(patches, grad)
+            full[...] = mm_nt(windows(h), grad)
         else:
-            full[...] += mm_nt(patches, grad)
+            full[...] += mm_nt(windows(h), grad)
 
     lane = lanes_of((16, 128))
     for r in range(3):
@@ -358,13 +392,6 @@
     chip, line = rank(0, gz, gy), rank(1, gz, gy)
     one_wait = share(0, lambda j: sg.at[j], sg_one, s_send.at[0], s_recv.at[0])
     sg_one[chip] = sg[chip]
-
-    turned = lax.dot_general(
-        chan_ref[...], jnp.concatenate(pooled, axis=1), (((0,), (0,)), ((), ())), preferred_element_type=F32
-    )
-    for half in range(2):
-        for chan in range(2):
-            pool_stage[:, chan * 2 + half, :] = turned[chan * 32 : chan * 32 + 32, half * 128 : half * 128 + 128]
 
     for h in range(2):
         pulled = mm(w2[...], grads[h])
@@ -452,14 +479,11 @@
     operands = [volume, first_weight, first_bias, second_weight, second_bias, upstream, *constants]
     results = pl.pallas_call(
         body,
-        out_shape=[
-            jax.ShapeDtypeStruct((2, 32, 256), BF16),
-            jax.ShapeDtypeStruct((32, 128), F32),
-            jax.ShapeDtypeStruct((16, 32, 128), SENT),
-        ],
-        in_specs=[VMEM] * len(operands),
+        out_shape=[mem((2, 32, 256), BF16), mem((32, 128), F32), mem((16, 32, 128), SENT)],
+        in_specs=[pl.BlockSpec(memory_space=pl.ANY)] * len(operands),
         out_specs=[VMEM] * 3,
         scratch_shapes=[
+            *[mem(x.shape, x.dtype) for x in operands], dma((10,)), mem((2, 256, 256), F32),
             mem((4, 64, 256), BF16), mem((10, 96, 256), BF16), mem((32, 4, 128), F32), mem((32, 4, 128), F32),
             mem((32, 4, 128), F32), mem((32, 4, 128), F32),
             mem((128, 32), F32), mem((256, 256), BF16), mem((1536, 256), BF16), mem((256, 1536), BF16),
@@ -481,7 +505,7 @@
         ],
         in_specs=[VMEM] * 3,
         out_specs=[VMEM] * 3,
-    )(*results)
+    )(*[pltpu.with_memory_space_constraint(x, pltpu.VMEM) for x in results])
 
 
 def solution(mesh):

time: 39 us -> 36.1 us (0.926)
  Pallas kernels: 38.2 us -> 35.3 us
    pallas_call x1, Pallas kernels: 36.4 us -> 34.5 us  [on_device(): pl.pallas_call(body, out_shape=[mem((2, 32, 256), BF16), mem((32, 128), F...]
    pallas_call x1, Pallas kernels: 1.83 us -> 0.89 us  [on_device(): pl.pallas_call(finish, out_shape=[jax.ShapeDtypeStruct((2, 32, 256), BF16...]
where the time goes in v5:
time: 36.1 us; the launch traced here: 36 us
  Pallas kernels  35.3 us (98%)
  between operations  0.64 us (2%)
    pallas_call x1, Pallas kernels, on_device(): pl.pallas_call(body, out_shape=[mem((2, 32, 256), BF16), mem((32, 128), F...  34.5 us
    pallas_call x1, Pallas kernels, on_device(): pl.pallas_call(finish, out_shape=[jax.ShapeDtypeStruct((2, 32, 256), BF16...  0.89 us

profile of v5, /device:TPU:1, one launch (start us, length us, event | category | flops | bytes accessed | tf_op | source)
XLA Modules:
  0.0 36.0 jit_solution(10453244937012817815)
XLA Ops:
  0.6 34.5 %shard_map.121 = (bf16[2,32,256]{2,1,0:T(8,128)(2,1)S(1)}, f32[32,128]{1,0:T(8,128)S(1)}, bf16[16,32,128]{2,1,0:T(8,128)(2,1)S(1)}) custom-call(bf16[4,4,16,256]{3,2,1,0:T(8,128)(2,1)} %vol_in.1, bf16[3,3,3,4,32]{4,3,2,1,0:T(4,128)(2,1)} %w1_in.1, f32[32]{0:T(128)} %b1_in.1, bf16[3,3,3,32,64]{4,3,2,1,0:T(8,128)(2,1)} %w2_in.1, f32[64]{0:T(128)} %b2_in.1, ...), custom_call_target="tpu_custom_call" | custom-call | tf_op jit(solution)/shard_map/pallas_call | solution.py:480
  35.1 0.9 %shard_map.122 = (bf16[2,32,256]{2,1,0:T(8,128)(2,1)}, f32[3,3,3,4,32]{4,3,2,1,0:T(4,128)}, f32[3,3,3,32,64]{4,3,2,1,0:T(8,128)}) custom-call(bf16[2,32,256]{2,1,0:T(8,128)(2,1)S(1)} %get-tuple-element.6.pool_in, f32[32,128]{1,0:T(8,128)S(1)} %get-tuple-element.7.first_in, bf16[16,32,128]{2,1,0:T(8,128)(2,1)S(1)} %get-tuple-element.8.second_in), custom_call_target="tpu_custom_call" | custom-call | tf_op jit(solution)/shard_map/pallas_call | solution.py:499

commit v6 on v5

--- a/solution.py
+++ b/solution.py
@@ -92,7 +92,11 @@
                         for t in range(3):
                             for c in range(4):
                                 out[pd, pr, pw, pd + r, pw + t, pr + s, c, ((r * 3 + s) * 3 + t) * 4 + c] = 1
-    return out.reshape(2048, 128).astype(jnp.bfloat16)
+    out = out.reshape(2048, 128)
+    mirrored = np.zeros_like(out)
+    for r in range(3):
+        mirrored[:, r * 36 : r * 36 + 36] = out[:, (2 - r) * 36 : (2 - r) * 36 + 36]
+    return np.stack([out, mirrored]).astype(jnp.bfloat16)
 
 
 def around(dz, dy):
@@ -100,10 +104,14 @@
     return lax.rem(gz + dz + GZ, GZ), lax.rem(gy + dy + GY, GY)
 
 
+def hops(offset):
+    x, y, z, core = offset
+    return min(x, 4 - x) + min(y, 4 - y) + min(z, 8 - z) + 0.5 * core
+
+
 def spread_order(kind):
     xs, ys, zs, cores = (range(n) for n in ((4, 4, 1, 1), (1, 1, 8, 2), (4, 4, 1, 2))[kind])
     all_ = [(x, y, z, c) for x in xs for y in ys for z in zs for c in cores]
-    hops = lambda o: min(o[0], 4 - o[0]) + min(o[1], 4 - o[1]) + min(o[2], 8 - o[2]) + 0.5 * o[3]
     return sorted([o for o in all_ if any(o)], key=lambda o: -hops(o))
 
 
@@ -161,13 +169,11 @@
         pl.semaphore_signal(barrier, inc=1, device_id=to, device_id_type=MESH)
 
     far = lax.rem(gz + 2 * lax.rem(gz, 2) - 1 + GZ, GZ)
-    for offset in spread_order(1):
-        if offset[2]:
-            tell(shifted(offset))
-    for offset in spread_order(2):
-        tell(shifted(offset))
     tell((far, lax.rem(gy + 1, GY)))
     tell((far, lax.rem(gy + GY - 1, GY)))
+    offsets = [o for o in spread_order(1) if o[2]] + spread_order(2)
+    for offset in sorted(offsets, key=lambda o: -hops(o)):
+        tell(shifted(offset))
 
     def wait():
         pl.semaphore_wait(barrier, 47)
@@ -192,22 +198,27 @@
     send, recv, a_send, a_recv, s_send, s_recv,
 ):
     gz, gy = place()
+    core = lax.rem(gz, 2)
+    near, far = gz + 1 - 2 * core, lax.rem(gz + 2 * core - 1 + GZ, GZ)
+    edge = (gz == 0) | (gz == GZ - 1)
+
+    def depth(d, count):
+        return jnp.where(core == 0, count - 1 - d, d)
+
     loads = []
     for source, target in (
-        (vol_in, vol_ref), (turn_in, turn_ref), (up_in, up_ref), (w1_in, w1_ref), (gather_in, gather_ref),
+        (vol_in, vol_ref), (turn_in, turn_ref), (up_in, up_ref), (w1_in, w1_ref), (gather_in.at[1 - core], gather_ref),
         (b1_in, b1_ref), (b2_in, b2_ref), (w2_in, w2_ref), (spread_in, spread_ref), (chan_in, chan_ref),
     ):
         loads.append(pltpu.make_async_copy(source, target, load.at[len(loads)]))
-    for one in loads[:3]:
-        one.start()
     greeted = greet()
-    for one in loads[3:]:
+    for one in loads:
         one.start()
     for one in loads[:3]:
         one.wait()
 
     for d in range(4):
-        flat = jnp.concatenate([vol_ref[c, d] for c in range(4)], axis=0)
+        flat = jnp.concatenate([vol_ref[c, depth(d, 4)] for c in range(4)], axis=0)
         own[d] = mm(turn_ref[...], flat).astype(BF16)
     for half in range(2):
         for chan in range(2):
@@ -227,11 +238,13 @@
     copies = []
 
     def send_halo():
-        for dz in (-1, 1, 0):
-            src_d, dst_d = {-1: (slice(0, 3), slice(7, 10)), 0: (slice(0, 4), slice(3, 7)), 1: (slice(1, 4), slice(0, 3))}[dz]
-            for dy in (-1, 1, 0):
-                if dz == 0 and dy == 0:
-                    continue
+        sides = (
+            (far, slice(1, 4), slice(7, 10), (1, -1, 0)),
+            (near, slice(0, 3), slice(0, 3), (1, -1, 0)),
+            (gz, slice(0, 4), slice(3, 7), (1, -1)),
+        )
+        for to, src_d, dst_d, steps in sides:
+            for dy in steps:
                 src_r, dst_r = {
                     -1: (slice(0, 16), slice(80, 96)),
                     0: (slice(0, 64), slice(16, 80)),
@@ -242,13 +255,13 @@
                     dst_ref=ext.at[dst_d, dst_r],
                     send_sem=send.at[len(copies)],
                     recv_sem=recv.at[len(copies)],
-                    device_id=around(dz, dy),
+                    device_id=(to, lax.rem(gy + dy + GY, GY)),
                     device_id_type=MESH,
                 )
                 copy.start()
                 copies.append(copy)
 
-    up_wait = share(2, lambda j: up_stage.at[j], up_got, a_send.at[0], a_recv.at[0], 10, send_halo)
+    up_wait = share(2, lambda j: up_stage.at[j], up_got, a_send.at[0], a_recv.at[0], 0, send_halo)
     for one in loads[7:]:
         one.wait()
 
@@ -259,48 +272,38 @@
             for s in range(4):
                 at = ((r * 3 + t) * 4 + s) * 32
                 for pd in range(2):
-                    near = w2_ref[r - pd, s, t].astype(F32) if 0 <= r - pd < 3 and s < 3 else None
-                    next_ = w2_ref[r - pd, s - 1, t].astype(F32) if 0 <= r - pd < 3 and s > 0 else None
-                    left = zero[:, :64] if near is None else near
+                    here = w2_ref[depth(r - pd, 3), s, t].astype(F32) if 0 <= r - pd < 3 and s < 3 else None
+                    next_ = w2_ref[depth(r - pd, 3), s - 1, t].astype(F32) if 0 <= r - pd < 3 and s > 0 else None
+                    left = zero[:, :64] if here is None else here
                     right = zero[:, :64] if next_ is None else next_
                     w2[at : at + 32, pd * 128 : pd * 128 + 128] = jnp.concatenate([left, right], axis=1).astype(BF16)
     w2_turned[...] = mm_nt(one_hot(256), w2[...]).astype(BF16)
 
-    ext[3:7, 16:80] = own[...]
-    for copy in copies:
-        copy.wait()
-
-    @pl.when(gz == 0)
-    def _():
-        ext[0:3] = jnp.zeros((3, 96, 256), BF16)
-
-    @pl.when(gz == GZ - 1)
-    def _():
-        ext[7:10] = jnp.zeros((3, 96, 256), BF16)
-
-    @pl.when(gy == 0)
-    def _():
-        ext[:, 0:16] = jnp.zeros((10, 16, 256), BF16)
-
-    @pl.when(gy == GY - 1)
-    def _():
-        ext[:, 80:96] = jnp.zeros((10, 16, 256), BF16)
-
-    flat = ext[...].reshape(960, 256)
-    for side in range(2):
-        wide = mm(flat, spread_ref[:, side * 256 : side * 256 + 256])
-        for k in range(2):
-            rows[:, 2 * side + k] = wide[:, k * 128 : k * 128 + 128].reshape(10, 96, 128)
+    def widen(value, targets, at):
+        many, high, _ = value.shape
+        flat = value.reshape(many * high, 256)
+        for side in range(2):
+            wide = mm(flat, spread_ref[:, side * 256 : side * 256 + 256])
+            for k in range(2):
+                for i, d in enumerate(targets):
+                    rows[d, 2 * side + k, at : at + high] = wide[i * high : i * high + high, k * 128 : k * 128 + 128]
+
+    def clear(deps, at):
+        ext[deps, at : at + 16] = jnp.zeros((deps.stop - deps.start, 16, 256), BF16)
 
     def inside(d, r):
-        ok = jnp.where(d == 0, gz > 0, jnp.where(d == 3, gz < GZ - 1, True))
-        if r == 0:
-            ok = ok & (gy > 0)
-        if r == 9:
-            ok = ok & (gy < GY - 1)
+        ok = None
+        if d == 3:
+            ok = jnp.logical_not(edge)
+        if r in (0, 9):
+            side = gy > 0 if r == 0 else gy < GY - 1
+            ok = side if ok is None else ok & side
         return ok
 
-    def layer_one(d, _):
+    def keep(ok, value):
+        return value if ok is None else jnp.where(ok, value, 0.0)
+
+    def layer_one(d):
         for dd in range(4):
             for dw in range(4):
                 for r in range(10):
@@ -317,28 +320,61 @@
             cell = (cell * 0.125).astype(BF16).astype(F32)
             for k in range(2):
                 r = 2 * j + k
-                one = jnp.where(inside(d, r), cell[:, k * 128 : k * 128 + 128], 0.0)
+                one = keep(inside(d, r), cell[:, k * 128 : k * 128 + 128])
                 act[d, 0, r * 32 : r * 32 + 32, :] = before(one).astype(BF16)
                 act[d, 1, r * 32 : r * 32 + 32, :] = one.astype(BF16)
                 act[d, 2, r * 32 : r * 32 + 32, :] = after(one).astype(BF16)
-        return 0
-
-    lax.fori_loop(0, 4, layer_one, 0, unroll=True)
-
-    lane = lanes_of((64, 128))
-    pooled = []
-
-    def windows(h):
+
+    def windows(h, deps):
         sides = []
         for k in range(2):
             r = 4 * h + 2 * k
-            sides.append(
-                jnp.concatenate([act[dd, dw, r * 32 : r * 32 + 128, :] for dd in range(4) for dw in range(3)], axis=0)
-            )
+            sides.append(jnp.concatenate([act[dd, dw, r * 32 : r * 32 + 128, :] for dd in deps for dw in range(3)], axis=0))
         return jnp.concatenate(sides, axis=1)
 
+    widen(own[...], (3, 4, 5, 6), 16)
+    for copy in copies[3:]:
+        copy.wait()
+
+    @pl.when(gy == 0)
+    def _():
+        clear(slice(0, 7), 0)
+
+    @pl.when(gy == GY - 1)
+    def _():
+        clear(slice(0, 7), 80)
+
+    widen(ext[0:3], (2, 1, 0), 0)
+    for at in (0, 80):
+        widen(ext[3:7, at : at + 16], (3, 4, 5, 6), at)
+    for d in range(2):
+        layer_one(d)
     for h in range(2):
-        value = mm(w2_turned[...], windows(h)) + b2
+        seen[h] = mm(w2_turned[:, :768], windows(h, (0, 1))) + b2
+
+    for copy in copies[:3]:
+        copy.wait()
+
+    @pl.when(gy == 0)
+    def _():
+        clear(slice(7, 10), 0)
+
+    @pl.when(gy == GY - 1)
+    def _():
+        clear(slice(7, 10), 80)
+
+    @pl.when(edge)
+    def _():
+        ext[7:10] = jnp.zeros((3, 96, 256), BF16)
+
+    widen(ext[7:10], (9, 8, 7), 0)
+    for d in range(2, 4):
+        layer_one(d)
+
+    lane = lanes_of((64, 128))
+    pooled = []
+    for h in range(2):
+        value = seen[h] + mm(w2_turned[:, 768:], windows(h, (2, 3)))
         seen[h] = value
         out = jnp.maximum(value, LEAK * value)
         cell = out[0:64] + out[64:128] + out[128:192] + out[192:256]
@@ -370,9 +406,9 @@
         )
         grads.append(grad)
         if h == 0:
-            full[...] = mm_nt(windows(h), grad)
+            full[...] = mm_nt(windows(h, range(4)), grad)
         else:
-            full[...] += mm_nt(windows(h), grad)
+            full[...] += mm_nt(windows(h, range(4)), grad)
 
     lane = lanes_of((16, 128))
     for r in range(3):
@@ -385,13 +421,12 @@
             for s in range(3):
                 low = near[s][:16] + pltpu.roll(near[s + 1][:16], 64, 1)
                 high = pltpu.roll(near[s][16:], 64, 1) + near[s + 1][16:]
-                at = (r * 3 + s) * 3 + t
-                sg[at // 2, (at % 2) * 16 : (at % 2) * 16 + 16, :] = jnp.where(lane < 64, low, high).astype(SENT)
-    sg[13, 16:32, :] = jnp.zeros((16, 128), SENT)
-    sg[14:16] = jnp.zeros((2, 32, 128), SENT)
+                at = (depth(r, 3) * 3 + s) * 3 + t
+                sg[pl.ds(pl.multiple_of(at * 16, 16), 16), :] = jnp.where(lane < 64, low, high).astype(SENT)
+    sg[432:512] = jnp.zeros((80, 128), SENT)
     chip, line = rank(0, gz, gy), rank(1, gz, gy)
-    one_wait = share(0, lambda j: sg.at[j], sg_one, s_send.at[0], s_recv.at[0])
-    sg_one[chip] = sg[chip]
+    one_wait = share(0, lambda j: sg.at[pl.ds(pl.multiple_of(j * 32, 32), 32)], sg_one, s_send.at[0], s_recv.at[0])
+    sg_one[chip] = sg[pl.ds(pl.multiple_of(chip * 32, 32), 32), :]
 
     for h in range(2):
         pulled = mm(w2[...], grads[h])
@@ -401,7 +436,7 @@
                 for k in range(2):
                     gact[dd, t, 2 * h + k] = pulled[at : at + 128, k * 128 : k * 128 + 128]
 
-    def layer_back(d, _):
+    def layer_back(d):
         for j in range(5):
             sides = []
             for k in range(2):
@@ -414,7 +449,7 @@
                             value = piece if value is None else value + piece
                     parts.append(value)
                 value = (after(parts[0]) + parts[1] + before(parts[2])) * 0.125
-                sides.append(jnp.where(inside(d, 2 * j + k), value, 0.0))
+                sides.append(keep(inside(d, 2 * j + k), value))
             strong = jnp.concatenate(sides, axis=1)
             weak = strong * LEAK
             seen = pre[d, :, j * 256 : j * 256 + 256].astype(F32)
@@ -422,10 +457,10 @@
                 [jnp.where(seen[g * 32 : g * 32 + 32] > 0, strong, weak).astype(BF16) for g in range(8)], axis=0
             )
             ffull[...] += mm_nt(grad, patch[d, :, j * 256 : j * 256 + 256])
-        return 0
 
     ffull[...] = jnp.zeros((256, 256), F32)
-    lax.fori_loop(0, 4, layer_back, 0, unroll=True)
+    for d in range(4):
+        layer_back(d)
     flat = jnp.concatenate([ffull[g * 32 : g * 32 + 32, :] for g in range(8)], axis=1)
     pieces = []
     for _ in range(3):
@@ -483,13 +518,13 @@
         in_specs=[pl.BlockSpec(memory_space=pl.ANY)] * len(operands),
         out_specs=[VMEM] * 3,
         scratch_shapes=[
-            *[mem(x.shape, x.dtype) for x in operands], dma((10,)), mem((2, 256, 256), F32),
+            *[mem(x.shape, x.dtype) for x in operands[:-1]], mem((2048, 128), BF16), dma((10,)), mem((2, 256, 256), F32),
             mem((4, 64, 256), BF16), mem((10, 96, 256), BF16), mem((32, 4, 128), F32), mem((32, 4, 128), F32),
             mem((32, 4, 128), F32), mem((32, 4, 128), F32),
             mem((128, 32), F32), mem((256, 256), BF16), mem((1536, 256), BF16), mem((256, 1536), BF16),
             mem((10, 4, 96, 128), F32), mem((4, 256, 1280), BF16), mem((4, 256, 1280), BF16), mem((4, 3, 320, 128), BF16),
             mem((1536, 256), F32), mem((4, 3, 4, 128, 128), F32), mem((256, 256), F32),
-            mem((16, 32, 128), SENT), mem((16, 32, 128), SENT), mem((32, 128), SENT), mem((16, 32, 128), SENT),
+            mem((512, 128), SENT), mem((16, 32, 128), SENT), mem((32, 128), SENT), mem((16, 32, 128), SENT),
             mem((16, 32, 128), SENT), mem((32, 128), SENT), mem((16, 32, 128), SENT), mem((32, 128), SENT),
             mem((16, 32, 128), SENT),
             dma((8,)), dma((8,)), dma((2,)), dma((2,)), dma((5,)), dma((5,)),

time: 36.1 us -> 35.1 us (0.972)
  Pallas kernels: 35.3 us -> 34.3 us
    pallas_call x1, Pallas kernels: 34.5 us -> 33.4 us  [on_device(): pl.pallas_call(body, out_shape=[mem((2, 32, 256), BF16), mem((32, 128), F...]
where the time goes in v6:
time: 35.1 us; the launch traced here: 35 us
  Pallas kernels  34.3 us (98%)
  between operations  0.64 us (2%)
    pallas_call x1, Pallas kernels, on_device(): pl.pallas_call(body, out_shape=[mem((2, 32, 256), BF16), mem((32, 128), F...  33.4 us
    pallas_call x1, Pallas kernels, on_device(): pl.pallas_call(finish, out_shape=[jax.ShapeDtypeStruct((2, 32, 256), BF16...  0.89 us

profile of v6, /device:TPU:1, one launch (start us, length us, event | category | flops | bytes accessed | tf_op | source)
XLA Modules:
  0.0 35.0 jit_solution(15951300233566387939)
XLA Ops:
  0.6 33.4 %shard_map.121 = (bf16[2,32,256]{2,1,0:T(8,128)(2,1)S(1)}, f32[32,128]{1,0:T(8,128)S(1)}, bf16[16,32,128]{2,1,0:T(8,128)(2,1)S(1)}) custom-call(bf16[4,4,16,256]{3,2,1,0:T(8,128)(2,1)} %vol_in.1, bf16[3,3,3,4,32]{4,3,2,1,0:T(4,128)(2,1)} %w1_in.1, f32[32]{0:T(128)} %b1_in.1, bf16[3,3,3,32,64]{4,3,2,1,0:T(8,128)(2,1)} %w2_in.1, f32[64]{0:T(128)} %b2_in.1, ...), custom_call_target="tpu_custom_call" | custom-call | tf_op jit(solution)/shard_map/pallas_call | solution.py:515
  34.1 0.9 %shard_map.122 = (bf16[2,32,256]{2,1,0:T(8,128)(2,1)}, f32[3,3,3,4,32]{4,3,2,1,0:T(4,128)}, f32[3,3,3,32,64]{4,3,2,1,0:T(8,128)}) custom-call(bf16[2,32,256]{2,1,0:T(8,128)(2,1)S(1)} %get-tuple-element.6.pool_in, f32[32,128]{1,0:T(8,128)S(1)} %get-tuple-element.7.first_in, bf16[16,32,128]{2,1,0:T(8,128)(2,1)S(1)} %get-tuple-element.8.second_in), custom_call_target="tpu_custom_call" | custom-call | tf_op jit(solution)/shard_map/pallas_call | solution.py:534

commit v7 on v6

--- a/solution.py
+++ b/solution.py
@@ -371,38 +371,23 @@
     for d in range(2, 4):
         layer_one(d)
 
-    lane = lanes_of((64, 128))
-    pooled = []
-    for h in range(2):
-        value = seen[h] + mm(w2_turned[:, 768:], windows(h, (2, 3)))
-        seen[h] = value
-        out = jnp.maximum(value, LEAK * value)
-        cell = out[0:64] + out[64:128] + out[128:192] + out[192:256]
-        left, right = cell[:, :128], cell[:, 128:]
-        left = left + pltpu.roll(left, 64, 1)
-        right = right + pltpu.roll(right, 64, 1)
-        pooled.append((jnp.where(lane < 64, left, right) * 0.125).astype(BF16))
-    turned = lax.dot_general(
-        chan_ref[...], jnp.concatenate(pooled, axis=1), (((0,), (0,)), ((), ())), preferred_element_type=F32
-    )
-    for half in range(2):
-        for chan in range(2):
-            pool_stage[:, chan * 2 + half, :] = turned[chan * 32 : chan * 32 + 32, half * 128 : half * 128 + 128]
-
     up_wait()
     up_got[gz] = up_stage[gz]
     wide = []
     for half in range(2):
         wide.append(jnp.concatenate([up_got[:, chan * 2 + half, :] for chan in range(2)], axis=0))
     back = mm(chan_ref[...], jnp.concatenate(wide, axis=1).astype(BF16))
+    lane = lanes_of((64, 128))
     grads = []
     for h in range(2):
+        value = seen[h] + mm(w2_turned[:, 768:], windows(h, (2, 3)))
+        seen[h] = value
         up = back[:, h * 128 : h * 128 + 128] * 0.125
         other = pltpu.roll(up, 64, 1)
         both = jnp.concatenate([jnp.where(lane < 64, up, other), jnp.where(lane < 64, other, up)], axis=1)
         weak = both * LEAK
         grad = jnp.concatenate(
-            [jnp.where(seen[h, g * 64 : g * 64 + 64] > 0, both, weak).astype(BF16) for g in range(4)], axis=0
+            [jnp.where(value[g * 64 : g * 64 + 64] > 0, both, weak).astype(BF16) for g in range(4)], axis=0
         )
         grads.append(grad)
         if h == 0:
@@ -427,6 +412,23 @@
     chip, line = rank(0, gz, gy), rank(1, gz, gy)
     one_wait = share(0, lambda j: sg.at[pl.ds(pl.multiple_of(j * 32, 32), 32)], sg_one, s_send.at[0], s_recv.at[0])
     sg_one[chip] = sg[pl.ds(pl.multiple_of(chip * 32, 32), 32), :]
+
+    lane = lanes_of((64, 128))
+    pooled = []
+    for h in range(2):
+        value = seen[h]
+        out = jnp.maximum(value, LEAK * value)
+        cell = out[0:64] + out[64:128] + out[128:192] + out[192:256]
+        left, right = cell[:, :128], cell[:, 128:]
+        left = left + pltpu.roll(left, 64, 1)
+        right = right + pltpu.roll(right, 64, 1)
+        pooled.append((jnp.where(lane < 64, left, right) * 0.125).astype(BF16))
+    turned = lax.dot_general(
+        chan_ref[...], jnp.concatenate(pooled, axis=1), (((0,), (0,)), ((), ())), preferred_element_type=F32
+    )
+    for half in range(2):
+        for chan in range(2):
+            pool_stage[:, chan * 2 + half, :] = turned[chan * 32 : chan * 32 + 32, half * 128 : half * 128 + 128]
 
     for h in range(2):
         pulled = mm(w2[...], grads[h])

time: 35.1 us -> 34.3 us (0.977)
  Pallas kernels: 34.3 us -> 33.6 us
    pallas_call x1, Pallas kernels: 33.4 us -> 32.7 us  [on_device(): pl.pallas_call(body, out_shape=[mem((2, 32, 256), BF16), mem((32, 128), F...]
where the time goes in v7:
time: 34.3 us; the launch traced here: 34.2 us
  Pallas kernels  33.6 us (98%)
  between operations  0.64 us (2%)
    pallas_call x1, Pallas kernels, on_device(): pl.pallas_call(body, out_shape=[mem((2, 32, 256), BF16), mem((32, 128), F...  32.7 us
    pallas_call x1, Pallas kernels, on_device(): pl.pallas_call(finish, out_shape=[jax.ShapeDtypeStruct((2, 32, 256), BF16...  0.89 us

profile of v7, /device:TPU:1, one launch (start us, length us, event | category | flops | bytes accessed | tf_op | source)
XLA Modules:
  0.0 34.2 jit_solution(4317846783775670776)
XLA Ops:
  0.6 32.7 %shard_map.121 = (bf16[2,32,256]{2,1,0:T(8,128)(2,1)S(1)}, f32[32,128]{1,0:T(8,128)S(1)}, bf16[16,32,128]{2,1,0:T(8,128)(2,1)S(1)}) custom-call(bf16[4,4,16,256]{3,2,1,0:T(8,128)(2,1)} %vol_in.1, bf16[3,3,3,4,32]{4,3,2,1,0:T(4,128)(2,1)} %w1_in.1, f32[32]{0:T(128)} %b1_in.1, bf16[3,3,3,32,64]{4,3,2,1,0:T(8,128)(2,1)} %w2_in.1, f32[64]{0:T(128)} %b2_in.1, ...), custom_call_target="tpu_custom_call" | custom-call | tf_op jit(solution)/shard_map/pallas_call | solution.py:517
  33.3 0.9 %shard_map.122 = (bf16[2,32,256]{2,1,0:T(8,128)(2,1)}, f32[3,3,3,4,32]{4,3,2,1,0:T(4,128)}, f32[3,3,3,32,64]{4,3,2,1,0:T(8,128)}) custom-call(bf16[2,32,256]{2,1,0:T(8,128)(2,1)S(1)} %get-tuple-element.6.pool_in, f32[32,128]{1,0:T(8,128)S(1)} %get-tuple-element.7.first_in, bf16[16,32,128]{2,1,0:T(8,128)(2,1)S(1)} %get-tuple-element.8.second_in), custom_call_target="tpu_custom_call" | custom-call | tf_op jit(solution)/shard_map/pallas_call | solution.py:536

commit v8 on v7

--- a/solution.py
+++ b/solution.py
@@ -261,7 +261,7 @@
                 copy.start()
                 copies.append(copy)
 
-    up_wait = share(2, lambda j: up_stage.at[j], up_got, a_send.at[0], a_recv.at[0], 0, send_halo)
+    up_wait = share(2, lambda j: up_stage.at[j], up_got, a_send.at[0], a_recv.at[0], 10, send_halo)
     for one in loads[7:]:
         one.wait()
 
@@ -390,10 +390,7 @@
             [jnp.where(value[g * 64 : g * 64 + 64] > 0, both, weak).astype(BF16) for g in range(4)], axis=0
         )
         grads.append(grad)
-        if h == 0:
-            full[...] = mm_nt(windows(h, range(4)), grad)
-        else:
-            full[...] += mm_nt(windows(h, range(4)), grad)
+        full[h] = mm_nt(windows(h, range(4)), grad)
 
     lane = lanes_of((16, 128))
     for r in range(3):
@@ -402,7 +399,11 @@
             for s in range(4):
                 a = ((r * 3 + t) * 4 + s) * 32
                 b = (((r + 1) * 3 + t) * 4 + s) * 32
-                near.append(full[a : a + 32, 0:128] + full[b : b + 32, 128:256])
+                near.append(
+                    full[0, a : a + 32, 0:128]
+                    + full[1, a : a + 32, 0:128]
+                    + (full[0, b : b + 32, 128:256] + full[1, b : b + 32, 128:256])
+                )
             for s in range(3):
                 low = near[s][:16] + pltpu.roll(near[s + 1][:16], 64, 1)
                 high = pltpu.roll(near[s][16:], 64, 1) + near[s + 1][16:]
@@ -492,16 +493,15 @@
         for chan in range(2):
             pool_out[chan, :, half * 128 : half * 128 + 128] = pool_got[:, chan * 2 + half, :].astype(BF16)
     t_wait()
-    first_out[...] = total16(t_two)
+    first_out[...] = jnp.transpose(total16(t_two))
     done_wait()
     second_out[...] = sg_done[...]
 
 
 def finish(pool_in, first_in, second_in, pool_out, first_out, second_out):
     pool_out[...] = pool_in[...]
-    turned = jnp.transpose(first_in[...])
     for i in range(27):
-        first_out[i // 9, i // 3 % 3, i % 3] = turned[4 * i : 4 * i + 4, :]
+        first_out[i // 9, i // 3 % 3, i % 3] = first_in[4 * i : 4 * i + 4, :]
         block = second_in[i // 2, (i % 2) * 16 : (i % 2) * 16 + 16, :].astype(F32)
         second_out[i // 9, i // 3 % 3, i % 3, 0:16, :] = block[:, :64]
         second_out[i // 9, i // 3 % 3, i % 3, 16:32, :] = block[:, 64:]
@@ -516,7 +516,7 @@
     operands = [volume, first_weight, first_bias, second_weight, second_bias, upstream, *constants]
     results = pl.pallas_call(
         body,
-        out_shape=[mem((2, 32, 256), BF16), mem((32, 128), F32), mem((16, 32, 128), SENT)],
+        out_shape=[mem((2, 32, 256), BF16), mem((128, 32), F32), mem((16, 32, 128), SENT)],
         in_specs=[pl.BlockSpec(memory_space=pl.ANY)] * len(operands),
         out_specs=[VMEM] * 3,
         scratch_shapes=[
@@ -525,7 +525,7 @@
             mem((32, 4, 128), F32), mem((32, 4, 128), F32),
             mem((128, 32), F32), mem((256, 256), BF16), mem((1536, 256), BF16), mem((256, 1536), BF16),
             mem((10, 4, 96, 128), F32), mem((4, 256, 1280), BF16), mem((4, 256, 1280), BF16), mem((4, 3, 320, 128), BF16),
-            mem((1536, 256), F32), mem((4, 3, 4, 128, 128), F32), mem((256, 256), F32),
+            mem((2, 1536, 256), F32), mem((4, 3, 4, 128, 128), F32), mem((256, 256), F32),
             mem((512, 128), SENT), mem((16, 32, 128), SENT), mem((32, 128), SENT), mem((16, 32, 128), SENT),
             mem((16, 32, 128), SENT), mem((32, 128), SENT), mem((16, 32, 128), SENT), mem((32, 128), SENT),
             mem((16, 32, 128), SENT),

time: 34.3 us -> 34.4 us (level)
  no operation moved by 1% of the time
where the time goes in v8:
time: 34.4 us; the launch traced here: 34.3 us
  Pallas kernels  33.6 us (98%)
  between operations  0.64 us (2%)
    pallas_call x1, Pallas kernels, on_device(): pl.pallas_call(body, out_shape=[mem((2, 32, 256), BF16), mem((128, 32), F...  32.8 us
    pallas_call x1, Pallas kernels, on_device(): pl.pallas_call(finish, out_shape=[jax.ShapeDtypeStruct((2, 32, 256), BF16...  0.86 us

profile of v8, /device:TPU:1, one launch (start us, length us, event | category | flops | bytes accessed | tf_op | source)
XLA Modules:
  0.0 34.3 jit_solution(4468229724728159610)
XLA Ops:
  0.6 32.8 %shard_map.121 = (bf16[2,32,256]{2,1,0:T(8,128)(2,1)S(1)}, f32[128,32]{1,0:T(8,128)S(1)}, bf16[16,32,128]{2,1,0:T(8,128)(2,1)S(1)}) custom-call(bf16[4,4,16,256]{3,2,1,0:T(8,128)(2,1)} %vol_in.1, bf16[3,3,3,4,32]{4,3,2,1,0:T(4,128)(2,1)} %w1_in.1, f32[32]{0:T(128)} %b1_in.1, bf16[3,3,3,32,64]{4,3,2,1,0:T(8,128)(2,1)} %w2_in.1, f32[64]{0:T(128)} %b2_in.1, ...), custom_call_target="tpu_custom_call" | custom-call | tf_op jit(solution)/shard_map/pallas_call | solution.py:517
  33.4 0.9 %shard_map.122 = (bf16[2,32,256]{2,1,0:T(8,128)(2,1)}, f32[3,3,3,4,32]{4,3,2,1,0:T(4,128)}, f32[3,3,3,32,64]{4,3,2,1,0:T(8,128)}) custom-call(bf16[2,32,256]{2,1,0:T(8,128)(2,1)S(1)} %get-tuple-element.6.pool_in, f32[128,32]{1,0:T(8,128)S(1)} %get-tuple-element.7.first_in, bf16[16,32,128]{2,1,0:T(8,128)(2,1)S(1)} %get-tuple-element.8.second_in), custom_call_target="tpu_custom_call" | custom-call | tf_op jit(solution)/shard_map/pallas_call | solution.py:536

commit v9 on v8

--- a/solution.py
+++ b/solution.py
@@ -239,7 +239,7 @@
 
     def send_halo():
         sides = (
-            (far, slice(1, 4), slice(7, 10), (1, -1, 0)),
+            (far, slice(1, 4), slice(7, 10), (0, 1, -1)),
             (near, slice(0, 3), slice(0, 3), (1, -1, 0)),
             (gz, slice(0, 4), slice(3, 7), (1, -1)),
         )
@@ -334,7 +334,7 @@
 
     widen(own[...], (3, 4, 5, 6), 16)
     for copy in copies[3:]:
-        copy.wait()
+        copy.wait_recv()
 
     @pl.when(gy == 0)
     def _():
@@ -353,7 +353,7 @@
         seen[h] = mm(w2_turned[:, :768], windows(h, (0, 1))) + b2
 
     for copy in copies[:3]:
-        copy.wait()
+        copy.wait_recv()
 
     @pl.when(gy == 0)
     def _():
@@ -489,6 +489,8 @@
     sg_done[chip] = total16(sg_two).astype(SENT)
     done_wait = share(0, lambda j: sg_done.at[chip], sg_done, s_send.at[2], s_recv.at[2])
     pool_wait()
+    for copy in copies:
+        copy.wait_send()
     for half in range(2):
         for chan in range(2):
             pool_out[chan, :, half * 128 : half * 128 + 128] = pool_got[:, chan * 2 + half, :].astype(BF16)

time: 34.4 us -> 34.4 us (level)
  no operation moved by 1% of the time
where the time goes in v9:
time: 34.4 us; the launch traced here: 34.3 us
  Pallas kernels  33.7 us (98%)
  between operations  0.64 us (2%)
    pallas_call x1, Pallas kernels, on_device(): pl.pallas_call(body, out_shape=[mem((2, 32, 256), BF16), mem((128, 32), F...  32.8 us
    pallas_call x1, Pallas kernels, on_device(): pl.pallas_call(finish, out_shape=[jax.ShapeDtypeStruct((2, 32, 256), BF16...  0.86 us

profile of v9, /device:TPU:1, one launch (start us, length us, event | category | flops | bytes accessed | tf_op | source)
XLA Modules:
  0.0 34.3 jit_solution(22560565163054732)
XLA Ops:
  0.6 32.8 %shard_map.121 = (bf16[2,32,256]{2,1,0:T(8,128)(2,1)S(1)}, f32[128,32]{1,0:T(8,128)S(1)}, bf16[16,32,128]{2,1,0:T(8,128)(2,1)S(1)}) custom-call(bf16[4,4,16,256]{3,2,1,0:T(8,128)(2,1)} %vol_in.1, bf16[3,3,3,4,32]{4,3,2,1,0:T(4,128)(2,1)} %w1_in.1, f32[32]{0:T(128)} %b1_in.1, bf16[3,3,3,32,64]{4,3,2,1,0:T(8,128)(2,1)} %w2_in.1, f32[64]{0:T(128)} %b2_in.1, ...), custom_call_target="tpu_custom_call" | custom-call | tf_op jit(solution)/shard_map/pallas_call | solution.py:519
  33.4 0.9 %shard_map.122 = (bf16[2,32,256]{2,1,0:T(8,128)(2,1)}, f32[3,3,3,4,32]{4,3,2,1,0:T(4,128)}, f32[3,3,3,32,64]{4,3,2,1,0:T(8,128)}) custom-call(bf16[2,32,256]{2,1,0:T(8,128)(2,1)S(1)} %get-tuple-element.6.pool_in, f32[128,32]{1,0:T(8,128)S(1)} %get-tuple-element.7.first_in, bf16[16,32,128]{2,1,0:T(8,128)(2,1)S(1)} %get-tuple-element.8.second_in), custom_call_target="tpu_custom_call" | custom-call | tf_op jit(solution)/shard_map/pallas_call | solution.py:538

commit v10 on v8

--- a/solution.py
+++ b/solution.py
@@ -486,8 +486,8 @@
     t_wait = share(1, lambda j: t_part, t_two, s_send.at[4], s_recv.at[4])
     t_two[line] = t_part[...]
     two_wait()
-    sg_done[chip] = total16(sg_two).astype(SENT)
-    done_wait = share(0, lambda j: sg_done.at[chip], sg_done, s_send.at[2], s_recv.at[2])
+    second_out[chip] = total16(sg_two).astype(SENT)
+    done_wait = share(0, lambda j: second_out.at[chip], second_out, s_send.at[2], s_recv.at[2])
     pool_wait()
     for half in range(2):
         for chan in range(2):
@@ -495,7 +495,6 @@
     t_wait()
     first_out[...] = jnp.transpose(total16(t_two))
     done_wait()
-    second_out[...] = sg_done[...]
 
 
 def finish(pool_in, first_in, second_in, pool_out, first_out, second_out):

time: 34.4 us -> 34.4 us (level)
  no operation moved by 1% of the time
where the time goes in v10:
time: 34.4 us; the launch traced here: 34.3 us
  Pallas kernels  33.6 us (98%)
  between operations  0.64 us (2%)
    pallas_call x1, Pallas kernels, on_device(): pl.pallas_call(body, out_shape=[mem((2, 32, 256), BF16), mem((128, 32), F...  32.8 us
    pallas_call x1, Pallas kernels, on_device(): pl.pallas_call(finish, out_shape=[jax.ShapeDtypeStruct((2, 32, 256), BF16...  0.86 us

profile of v10, /device:TPU:1, one launch (start us, length us, event | category | flops | bytes accessed | tf_op | source)
XLA Modules:
  0.0 34.3 jit_solution(11917252310008336493)
XLA Ops:
  0.6 32.8 %shard_map.121 = (bf16[2,32,256]{2,1,0:T(8,128)(2,1)S(1)}, f32[128,32]{1,0:T(8,128)S(1)}, bf16[16,32,128]{2,1,0:T(8,128)(2,1)S(1)}) custom-call(bf16[4,4,16,256]{3,2,1,0:T(8,128)(2,1)} %vol_in.1, bf16[3,3,3,4,32]{4,3,2,1,0:T(4,128)(2,1)} %w1_in.1, f32[32]{0:T(128)} %b1_in.1, bf16[3,3,3,32,64]{4,3,2,1,0:T(8,128)(2,1)} %w2_in.1, f32[64]{0:T(128)} %b2_in.1, ...), custom_call_target="tpu_custom_call" | custom-call | tf_op jit(solution)/shard_map/pallas_call | solution.py:516
  33.4 0.9 %shard_map.122 = (bf16[2,32,256]{2,1,0:T(8,128)(2,1)}, f32[3,3,3,4,32]{4,3,2,1,0:T(4,128)}, f32[3,3,3,32,64]{4,3,2,1,0:T(8,128)}) custom-call(bf16[2,32,256]{2,1,0:T(8,128)(2,1)S(1)} %get-tuple-element.6.pool_in, f32[128,32]{1,0:T(8,128)S(1)} %get-tuple-element.7.first_in, bf16[16,32,128]{2,1,0:T(8,128)(2,1)S(1)} %get-tuple-element.8.second_in), custom_call_target="tpu_custom_call" | custom-call | tf_op jit(solution)/shard_map/pallas_call | solution.py:535
